TPU v7x, 32 devices: a whole 2x2x4 slice. The times are simulated.
32 devices in a mesh: groups: 2 (over x), dp: 16 (over z, y, core).
Axes of the slice: x: 2, y: 2, z: 4, core: 2. Of those that a mesh axis runs over, the one named last changes fastest.
Arguments:
- tokens: bfloat16 [128, 4096], P(('groups', 'dp')), parts along dimension 0, may hold values from -6 to 6
- target: bfloat16 [128, 4096], P(('groups', 'dp')), parts along dimension 0, may hold values from -3 to 3
- w_gate: bfloat16 [4096, 4096], P('dp'), may hold values from -0.09375 to 0.09375
- w_up: bfloat16 [4096, 4096], P('dp'), may hold values from -0.09375 to 0.09375
- w_down_t: bfloat16 [4096, 4096], P('dp'), may hold values from -0.09375 to 0.09375
- kept_blocks: int32 [30], replicated, may hold values from 0 to 31, as said below
Outputs:
- grad_gate: bfloat16 [8192, 3840], P('groups', 'dp'), parts along dimension 0
- grad_up: bfloat16 [8192, 3840], P('groups', 'dp'), parts along dimension 0
- grad_down: bfloat16 [8192, 3840], P('groups', 'dp'), parts along dimension 0
There are 2 independent parts, one for each index of `groups`. A program takes and returns all parts, laid end to end along the dimension named above; an argument that names none is the same for every part. Nothing has to cross between parts.
Inputs may be any that keep to these rules, and one draw needn't show every extreme that they name: `kept_blocks`: distinct teacher block numbers in increasing order; blocks 0 and 31 are always kept.
All inputs are finite; a program needn't handle non-finite values.
Results may differ from a plain program's by a relative error of at most 0.0064.
Values may be sent and summed in bfloat16 or wider, within the bound.
A program may use at most 128 MiB of HBM per device.

v0:
```python
import jax
import jax.numpy as jnp
from jax import lax
from jax.sharding import PartitionSpec as P

BLK = 128


LOSS_SCALE = 16.0


def channel_index(kept_blocks):
    offsets = jnp.arange(BLK, dtype=jnp.int32)
    return (kept_blocks[:, None] * BLK + offsets[None, :]).reshape(-1)


def body(tokens, target, w_gate, w_up, w_down_t, kept_blocks):
    channels = channel_index(kept_blocks)
    picked_gate = jnp.take(w_gate, channels, axis=1)
    picked_up = jnp.take(w_up, channels, axis=1)
    picked_down = jnp.take(w_down_t, channels, axis=1)
    student_gate, student_up, student_down = (
        lax.all_to_all(picked_gate, "dp", split_axis=1, concat_axis=0, tiled=True),
        lax.all_to_all(picked_up, "dp", split_axis=1, concat_axis=0, tiled=True),
        lax.all_to_all(picked_down, "dp", split_axis=1, concat_axis=0, tiled=True),
    )
    gathered = lax.all_gather(tokens, "dp", axis=0, tiled=True)
    scale = LOSS_SCALE / gathered.shape[0]
    gate_act = jnp.dot(gathered, student_gate, preferred_element_type=jnp.float32)
    up_act = jnp.dot(gathered, student_up, preferred_element_type=jnp.float32)
    sigmoid_gate = jax.nn.sigmoid(gate_act)
    silu_gate = gate_act * sigmoid_gate
    hidden = (silu_gate * up_act).astype(jnp.bfloat16)
    output_rows = lax.psum_scatter(
        lax.dot_general(
            hidden, student_down, (((1,), (1,)), ((), ())), preferred_element_type=jnp.float32
        ),
        "dp",
        scatter_dimension=0,
        tiled=True,
    )
    residual = ((output_rows - target.astype(jnp.float32)) * scale).astype(jnp.bfloat16)
    residual_all = lax.all_gather(residual, "dp", axis=0, tiled=True)
    grad_down = lax.dot_general(
        residual_all, hidden, (((0,), (0,)), ((), ())), preferred_element_type=jnp.float32
    )
    hidden_grad = jnp.dot(residual_all, student_down, preferred_element_type=jnp.float32)
    slope = sigmoid_gate * (1.0 + gate_act * (1.0 - sigmoid_gate))
    gate_grad = (hidden_grad * up_act * slope).astype(jnp.bfloat16)
    up_grad = (hidden_grad * silu_gate).astype(jnp.bfloat16)
    grad_gate = lax.dot_general(
        gathered, gate_grad, (((0,), (0,)), ((), ())), preferred_element_type=jnp.float32
    )
    grad_up = lax.dot_general(
        gathered, up_grad, (((0,), (0,)), ((), ())), preferred_element_type=jnp.float32
    )
    return (
        grad_gate.astype(jnp.bfloat16),
        grad_up.astype(jnp.bfloat16),
        grad_down.astype(jnp.bfloat16),
    )


def solution(mesh):
    placed = (
        P(("groups", "dp"), None),
        P(("groups", "dp"), None),
        P("dp", None),
        P("dp", None),
        P("dp", None),
        P(),
    )
    return jax.shard_map(
        body,
        mesh=mesh,
        in_specs=placed,
        out_specs=(P("groups", "dp"), P("groups", "dp"), P("groups", "dp")),
        check_vma=False,
    )
```

profile of v0, /device:TPU:0, one launch (start us, length us, event | category | flops | bytes accessed | tf_op | source)
XLA Modules:
  0.0 363.7 jit_solution(11824803540052855395)
XLA Ops:
  7.2 0.7 broadcast_multiply_fusion
  7.8 0.1 compare_select_fusion
  7.9 0.1 compare_and_fusion
  8.0 4.1 %copy.18 = bf16[256,4096]{0,1:T(8,128)(2,1)} copy(bf16[256,4096]{1,0:T(8,128)(2,1)} %param.10) | data formatting | bytes 4194304 | tf_op args[2]
  12.1 3.3 copy.20
  15.4 11.6 %gather_fusion = bf16[3840,256]{1,0:T(8,128)(2,1)} fusion(bf16[256,4096]{0,1:T(8,128)(2,1)} %copy.18, s32[4096]{0:T(1024)S(1)} %pad_clamp_fusion), kind=kCustom, calls=%fused_computation.clone | custom fusion | bytes 3947520 | tf_op jit(solution)/shard_map/jit(_take)/gather | solution.py:19
  26.9 11.6 %gather_fusion.1 = bf16[3840,256]{1,0:T(8,128)(2,1)} fusion(bf16[256,4096]{0,1:T(8,128)(2,1)S(1)} %copy.20, s32[4096]{0:T(1024)S(1)} %pad_clamp_fusion), kind=kCustom, calls=%fused_computation.1.clone | custom fusion | bytes 3947520 | tf_op jit(solution)/shard_map/jit(_take)/gather | solution.py:20
  38.5 3.3 copy.22
  41.8 11.6 %gather_fusion.2 = bf16[3840,256]{1,0:T(8,128)(2,1)} fusion(bf16[256,4096]{0,1:T(8,128)(2,1)S(1)} %copy.22, s32[4096]{0:T(1024)S(1)} %pad_clamp_fusion), kind=kCustom, calls=%fused_computation.2.clone | custom fusion | bytes 3947520 | tf_op jit(solution)/shard_map/jit(_take)/gather | solution.py:21
  53.4 4.7 %broadcast_select_fusion = (bf16[3840,256]{1,0:T(8,128)(2,1)}, bf16[3840,256]{1,0:T(8,128)(2,1)S(1)}, bf16[3840,256]{1,0:T(8,128)(2,1)S(1)}) fusion(bf16[3840,256]{1,0:T(8,128)(2,1)} %gather_fusion.2, pred[3840]{0:T(1024)(128)(4,1)S(1)} %compare_and_fusion, bf16[3840,256]{1,0:T(8,128)(2,1)} %gather_fusion.1, bf16[3840,256]{1,0:T(8,128)(2,1)} %gather_fusion), kind=kLoop, calls=%fused_computation.8 | loop fusion | flops 2949120 | bytes 11800320 | tf_op jit(solution)/shard_map/jit(_take)/select_n | solution.py:21
  58.1 52.3 %all_to_all.57 = bf16[256,16,240]{0,2,1:T(8,128)(2,1)} all-to-all(bf16[256,16,240]{0,2,1:T(8,128)(2,1)S(1)} %bitcast.54), channel_id=1, replica_groups=mesh['groups'=2,'dp'=16] {'dp'}, dimensions={1} | all-to-all | bytes 3932160 | tf_op jit(solution)/shard_map/all_to_all | solution.py:23
  110.4 49.5 %all_to_all.58 = bf16[256,16,240]{0,2,1:T(8,128)(2,1)} all-to-all(bf16[256,16,240]{0,2,1:T(8,128)(2,1)S(1)} %bitcast.53), channel_id=1, replica_groups=mesh['groups'=2,'dp'=16] {'dp'}, dimensions={1} | all-to-all | bytes 3932160 | tf_op jit(solution)/shard_map/all_to_all | solution.py:24
  159.9 4.7 %all-to-all-start.2 = ((bf16[256,16,240]{0,2,1:T(8,128)(2,1)}), bf16[256,16,240]{0,2,1:T(8,128)(2,1)S(1)}, u32[]{:S(2)}, u32[]{:S(2)}) async-start(bf16[256,16,240]{0,2,1:T(8,128)(2,1)} %bitcast.11), calls=%async_computation.2 | async-start | bytes 3932160 | tf_op jit(solution)/shard_map/all_to_all | solution.py:25
  164.6 0.0 all-reduce.3.cloned.1.call-start
  164.6 0.0 copy-done.8
  164.7 53.8 %all-gather = bf16[16,4,4096]{2,1,0:T(4,128)(2,1)S(1)} all-gather(bf16[1,4,4096]{2,1,0:T(4,128)(2,1)S(1)} %bitcast.55), channel_id=1, replica_groups=mesh['groups'=2,'dp'=16] {'dp'}, dimensions={0}, use_global_device_ids=true | all-gather | bytes 557056 | tf_op jit(solution)/shard_map/all_gather | solution.py:27
  218.5 0.1 reshape.54
  218.6 0.0 copy-start.1
  218.6 3.2 copy.24
  221.8 0.0 copy-done.1
  221.8 1.5 copy.25
  223.3 0.0 all-to-all-done.2
  223.3 1.3 copy-done
  224.6 1.9 copy.26
  226.5 0.0 copy-start.2
  226.5 0.2 copy-done.3
  226.7 0.7 convolution_bitcast_fusion.1
  227.4 0.0 copy-start.4
  227.5 0.7 copy-done.2
  228.1 1.4 multiply_convert_fusion.2
  229.5 0.0 copy-done.4
  229.5 0.6 copy-done.6
  230.1 1.4 fusion.10
  231.5 0.0 all-reduce.3.cloned.1.call-update
  231.5 0.0 copy-done.10
  231.5 0.7 dynamic-slice
  232.9 94.3 %all-reduce.3.cloned.1.call-done = f32[64,4096]{1,0:T(8,128)} async-done(((f32[64,4096]{1,0:T(8,128)}), f32[64,4096]{1,0:T(8,128)}) %all-reduce.3.cloned.1.call-update) | async-done | bytes 1048592
  327.2 0.0 copy-done.9
  327.2 0.9 fusion.5
  328.1 21.1 %all-gather.1 = bf16[16,4,4096]{2,1,0:T(4,128)(2,1)S(1)} all-gather(bf16[1,4,4096]{2,1,0:T(4,128)(2,1)S(1)} %fusion.5), channel_id=1, replica_groups=mesh['groups'=2,'dp'=16] {'dp'}, dimensions={0}, use_global_device_ids=true | all-gather | bytes 557056 | tf_op jit(solution)/shard_map/all_gather | solution.py:43
  349.2 0.1 reshape.56
  349.3 0.0 copy-start.5
  349.4 2.8 convolution_convert_fusion
  352.1 0.7 fusion.11
  352.8 0.0 copy-done.5
  352.9 2.0 fusion.1
  354.8 0.0 copy-done.7
  354.8 2.0 fusion
  (8 shorter events, 0.0 us)
Async XLA Ops:
  159.9 4.7 %copy-start.8 = (bf16[4,4096]{1,0:T(4,128)(2,1)S(1)}, bf16[4,4096]{1,0:T(4,128)(2,1)}, u32[]{:S(2)}) copy-start(bf16[4,4096]{1,0:T(4,128)(2,1)} %param.8) | copy-start | bytes 98308
  159.9 63.4 %all-to-all-start.2 = ((bf16[256,16,240]{0,2,1:T(8,128)(2,1)}), bf16[256,16,240]{0,2,1:T(8,128)(2,1)S(1)}, u32[]{:S(2)}, u32[]{:S(2)}) async-start(bf16[256,16,240]{0,2,1:T(8,128)(2,1)} %bitcast.11), calls=%async_computation.2 | async-start | bytes 3932160 | tf_op jit(solution)/shard_map/all_to_all | solution.py:25
  164.6 162.6 %all-reduce.3.cloned.1.call-start = ((), (), s32[]{:S(2)}) async-start(), calls=%async_computation.3 | async-start | bytes 2097152
  218.6 3.2 copy-start.1
  223.3 1.3 copy-start
  224.6 2.1 copy-start.3
  226.5 1.6 copy-start.2
  227.4 2.0 copy-start.4
  229.5 0.6 copy-start.6
  230.1 1.5 copy-start.10
  230.1 97.1 %copy-start.9 = (bf16[4,4096]{1,0:T(4,128)(2,1)S(1)}, bf16[4,4096]{1,0:T(4,128)(2,1)}, u32[]{:S(2)}) copy-start(bf16[4,4096]{1,0:T(4,128)(2,1)} %param.9) | copy-start | bytes 98308
  349.3 3.5 copy-start.5
  352.1 2.7 copy-start.7
Sparse Core Ops, SparseCore 0:
  231.7 95.4 all-reduce.2
where the time goes:
time: 364 us
  blocking collectives  177 us (49%)
  waiting for transfers between devices  94.3 us (26%)
  local copies, waits for them, and re-layouts  55.7 us (15%)
  between operations  14.8 us (4%)
  matrix products  11 us (3%)
  other arithmetic  6.43 us (2%)
  starting transfers between devices  4.72 us (1%)
    unnamed x2, waiting for transfers between devices  94.3 us
    all_gather x1, blocking collectives, body(): gathered = lax.all_gather(tokens, 'dp', axis=0, tiled=True)  53.8 us
    all_to_all x1, blocking collectives, body(): lax.all_to_all(picked_gate, 'dp', split_axis=1, concat_axis=0, tiled=True)  52.3 us
    all_to_all x1, blocking collectives, body(): lax.all_to_all(picked_up, 'dp', split_axis=1, concat_axis=0, tiled=True)  49.5 us
    all_gather x1, blocking collectives, body(): residual_all = lax.all_gather(residual, 'dp', axis=0, tiled=True)  21.1 us
    unnamed x28, local copies, waits for them, and re-layouts  14.3 us
    gather x1, local copies, waits for them, and re-layouts, body(): picked_down = jnp.take(w_down_t, channels, axis=1)  11.6 us
    gather x1, local copies, waits for them, and re-layouts, body(): picked_up = jnp.take(w_up, channels, axis=1)  11.6 us
  transfers between devices with their start and end apart: 2, of which 1 were waited for; matrix products, arithmetic and copies ran while one was open for 2% of the time, Pallas kernels for 0%

commit v1 on v0

--- a/solution.py
+++ b/solution.py
@@ -14,7 +14,7 @@
     return (kept_blocks[:, None] * BLK + offsets[None, :]).reshape(-1)
 
 
-def body(tokens, target, w_gate, w_up, w_down_t, kept_blocks):
+def gathered_weights_body(tokens, target, w_gate, w_up, w_down_t, kept_blocks):
     channels = channel_index(kept_blocks)
     picked_gate = jnp.take(w_gate, channels, axis=1)
     picked_up = jnp.take(w_up, channels, axis=1)
@@ -61,6 +61,73 @@
     )
 
 
+def select_blocks(full, kept_blocks):
+    rows, width = full.shape
+    blocks = full.reshape(rows, width // BLK, BLK)
+    return jnp.take(blocks, kept_blocks, axis=1, mode="clip").reshape(rows, -1)
+
+
+def resident_weights_body(tokens, target, w_gate, w_up, w_down_t, kept_blocks):
+    parts = lax.axis_size("dp")
+    me = lax.axis_index("dp")
+    features = w_gate.shape[0]
+    held = kept_blocks.shape[0] * BLK // parts
+    gathered = lax.all_gather(tokens, "dp", axis=0, tiled=True)
+    rows = gathered.shape[0]
+    target_slice = lax.all_to_all(target, "dp", split_axis=1, concat_axis=0, tiled=True)
+    scale = LOSS_SCALE / rows
+    token_slice = lax.dynamic_slice_in_dim(gathered, me * features, features, axis=1)
+
+    def partial(left, weight):
+        full = jnp.dot(left, weight, preferred_element_type=jnp.float32)
+        picked = select_blocks(full.astype(jnp.bfloat16), kept_blocks)
+        return picked.reshape(rows, parts, held).transpose(1, 0, 2)
+
+    def add_up(pieces):
+        moved = lax.all_to_all(pieces, "dp", split_axis=0, concat_axis=0, tiled=True)
+        return jnp.sum(moved.astype(jnp.float32), axis=0)
+
+    both = add_up(
+        jnp.concatenate([partial(token_slice, w_gate), partial(token_slice, w_up)], axis=1)
+    )
+    gate_act, up_act = both[:rows], both[rows:]
+    sigmoid_gate = jax.nn.sigmoid(gate_act)
+    silu_gate = gate_act * sigmoid_gate
+    hidden = (silu_gate * up_act).astype(jnp.bfloat16)
+    hidden_all = lax.all_gather(hidden, "dp", axis=1, tiled=True)
+    student_down = select_blocks(w_down_t, kept_blocks)
+    output = lax.dot_general(
+        hidden_all, student_down, (((1,), (1,)), ((), ())), preferred_element_type=jnp.float32
+    )
+    residual = ((output - target_slice.astype(jnp.float32)) * scale).astype(jnp.bfloat16)
+    residual_all = lax.all_gather(residual, "dp", axis=1, tiled=True)
+    hidden_grad = add_up(partial(residual, w_down_t))
+    grad_down = lax.dot_general(
+        residual_all, hidden, (((0,), (0,)), ((), ())), preferred_element_type=jnp.float32
+    )
+    slope = sigmoid_gate * (1.0 + gate_act * (1.0 - sigmoid_gate))
+    gate_grad = (hidden_grad * up_act * slope).astype(jnp.bfloat16)
+    up_grad = (hidden_grad * silu_gate).astype(jnp.bfloat16)
+    grad_gate = lax.dot_general(
+        gathered, gate_grad, (((0,), (0,)), ((), ())), preferred_element_type=jnp.float32
+    )
+    grad_up = lax.dot_general(
+        gathered, up_grad, (((0,), (0,)), ((), ())), preferred_element_type=jnp.float32
+    )
+    return (
+        grad_gate.astype(jnp.bfloat16),
+        grad_up.astype(jnp.bfloat16),
+        grad_down.astype(jnp.bfloat16),
+    )
+
+
+def body(tokens, target, w_gate, w_up, w_down_t, kept_blocks):
+    token_rows = tokens.shape[0] * lax.axis_size("dp")
+    few_tokens = token_rows < w_gate.shape[0]
+    chosen = resident_weights_body if few_tokens else gathered_weights_body
+    return chosen(tokens, target, w_gate, w_up, w_down_t, kept_blocks)
+
+
 def solution(mesh):
     placed = (
         P(("groups", "dp"), None),

time: 364 us -> 152 us (0.42)
  blocking collectives: 177 us -> 74 us
  waiting for transfers between devices: 94.3 us -> 6.04 us
  local copies, waits for them, and re-layouts: 55.7 us -> 39.9 us
  between operations: 14.8 us -> 0.81 us
  starting transfers between devices: 4.72 us -> 15.4 us
    all_to_all x2 -> x0, blocking collectives: 102 us -> none  [the longest x1 52.3 us: body(): lax.all_to_all(picked_gate, 'dp', split_axis=1, concat_axis=0, tiled=True)]
    unnamed x2 -> x0, waiting for transfers between devices: 94.3 us -> none
    gather x3 -> x8, local copies, waits for them, and re-layouts: 34.8 us -> 16 us  [select_blocks(): return jnp.take(blocks, kept_blocks, axis=1, mode='clip').reshape(rows, -1)]
    all_to_all x1 -> x3, starting transfers between devices: 4.67 us -> 15.4 us  [the longest x2 7.89 us: add_up(): lax.all_to_all(pieces, 'dp', split_axis=0, concat_axis=0, tiled=True)]
    unnamed x28 -> x10, local copies, waits for them, and re-layouts: 14.3 us -> 5.87 us
    another operation x0 -> x3, local copies, waits for them, and re-layouts: none -> 7.05 us  [partial(): return picked.reshape(rows, parts, held).transpose(1, 0, 2)]
    reshape x0 -> x4, local copies, waits for them, and re-layouts: none -> 6.9 us  [select_blocks(): blocks = full.reshape(rows, width // BLK, BLK)]
    all_to_all x3 -> x0, local copies, waits for them, and re-layouts: 6.62 us -> none  [the longest x1 3.2 us: body(): lax.all_to_all(picked_gate, 'dp', split_axis=1, concat_axis=0, tiled=True)]
  transfers between devices with their start and end apart: 2 -> 3, of which waited for: 1 -> 1; matrix products, arithmetic and copies ran while one was open for 2% -> 25% of each run, Pallas kernels for 0% -> 0%
where the time goes in v1:
time: 152 us; the launch traced here: 151 us
  blocking collectives  74 us (49%)
  local copies, waits for them, and re-layouts  39.9 us (26%)
  starting transfers between devices  15.4 us (10%)
  matrix products  11.3 us (7%)
  waiting for transfers between devices  6.04 us (4%)
  other arithmetic  3.73 us (2%)
    all_gather x1, blocking collectives, resident_weights_body(): residual_all = lax.all_gather(residual, 'dp', axis=1, tiled=True)  26.8 us
    all_gather x1, blocking collectives, resident_weights_body(): hidden_all = lax.all_gather(hidden, 'dp', axis=1, tiled=True)  23.7 us
    all_gather x1, blocking collectives, resident_weights_body(): gathered = lax.all_gather(tokens, 'dp', axis=0, tiled=True)  23.5 us
    gather x8, local copies, waits for them, and re-layouts, select_blocks(): return jnp.take(blocks, kept_blocks, axis=1, mode='clip').reshape(rows, -1)  16 us
    all_to_all x2, starting transfers between devices, add_up(): lax.all_to_all(pieces, 'dp', split_axis=0, concat_axis=0, tiled=True)  7.89 us
    all_to_all x1, starting transfers between devices, resident_weights_body(): lax.all_to_all(target, 'dp', split_axis=1, concat_axis=0, tiled=True)  7.53 us
    another operation x3, local copies, waits for them, and re-layouts, partial(): return picked.reshape(rows, parts, held).transpose(1, 0, 2)  7.05 us
    reshape x4, local copies, waits for them, and re-layouts, select_blocks(): blocks = full.reshape(rows, width // BLK, BLK)  6.9 us
  transfers between devices with their start and end apart: 3, of which 1 were waited for; matrix products, arithmetic and copies ran while one was open for 25% of the time, Pallas kernels for 0%

profile of v1, /device:TPU:0, one launch (start us, length us, event | category | flops | bytes accessed | tf_op | source)
XLA Modules:
  0.0 151.1 jit_solution(16462777891579633328)
XLA Ops:
  0.6 0.0 copy-start
  0.6 7.5 %all-to-all-start.1 = ((bf16[4,16,256]{2,0,1:T(4,128)(2,1)}), bf16[4,16,256]{2,0,1:T(4,128)(2,1)S(1)}, u32[]{:S(2)}, u32[]{:S(2)}) async-start(bf16[4,16,256]{2,0,1:T(4,128)(2,1)} %bitcast.61), calls=%async_computation.1 | async-start | bytes 65536 | tf_op jit(solution)/shard_map/all_to_all | solution.py:77
  8.2 23.5 %all-gather = bf16[16,4,4096]{2,1,0:T(4,128)(2,1)S(1)} all-gather(bf16[1,4,4096]{2,1,0:T(4,128)(2,1)} %bitcast.60), channel_id=1, replica_groups=mesh['groups'=2,'dp'=16] {'dp'}, dimensions={0}, use_global_device_ids=true | all-gather | bytes 557056 | tf_op jit(solution)/shard_map/all_gather | solution.py:75
  31.6 0.1 reshape.69
  31.8 0.0 copy-start.2
  31.8 0.0 copy-done
  31.8 0.5 fusion.2
  32.3 0.9 copy.80
  33.2 0.0 copy-done.2
  33.2 1.7 %gather_fusion = bf16[30,64,128]{2,1,0:T(8,128)(2,1)S(1)} fusion(bf16[64,32,128]{2,0,1:T(8,128)(2,1)} %bitcast.53, s32[1024]{0:T(1024)S(1)} %pad_clamp_fusion), kind=kCustom, calls=%fused_computation | custom fusion | bytes 983160 | tf_op jit(solution)/shard_map/jit(_take)/gather | solution.py:67
  34.9 1.1 copy.57
  36.0 2.9 %reshape_reshape.9 = bf16[64,16,240]{2,1,0:T(8,128)(2,1)} reshape(bf16[64,30,128]{2,1,0:T(8,128)(2,1)} %copy.57) | data formatting | bytes 983040 | tf_op jit(solution)/shard_map/reshape;reshape | solution.py:84
  38.9 2.1 %fusion.3 = bf16[8,32,8,128]{3,2,1,0:T(8,128)(2,1)S(1)} fusion(bf16[256,4096]{1,0:T(8,128)(2,1)} %param.9, bf16[64,4096]{1,0:T(8,128)(2,1)S(1)} %reshape.69, s32[]{:T(128)S(6)} %select_n.3), kind=kOutput, calls=%fused_computation.14 | convolution fusion | flops 134479872 | bytes 2654212 | tf_op jit(solution)/shard_map/dot_general | solution.py:82
  41.0 0.9 copy.79
  41.9 1.7 %gather_fusion.1 = bf16[30,64,128]{2,1,0:T(8,128)(2,1)S(1)} fusion(bf16[64,32,128]{2,0,1:T(8,128)(2,1)} %bitcast.55, s32[1024]{0:T(1024)S(1)} %pad_clamp_fusion), kind=kCustom, calls=%fused_computation.1 | custom fusion | bytes 983160 | tf_op jit(solution)/shard_map/jit(_take)/gather | solution.py:67
  43.6 1.1 copy.59
  44.7 2.1 %reshape_reshape.10 = bf16[64,16,240]{2,1,0:T(8,128)(2,1)S(1)} reshape(bf16[64,30,128]{2,1,0:T(8,128)(2,1)} %copy.59) | data formatting | bytes 983040 | tf_op jit(solution)/shard_map/reshape;reshape | solution.py:84
  46.8 2.2 %pad_maximum_fusion = bf16[16,128,240]{2,0,1:T(8,128)(2,1)} fusion(bf16[16,64,240]{2,0,1:T(8,128)(2,1)S(1)} %bitcast.58, bf16[16,64,240]{2,0,1:T(8,128)(2,1)} %bitcast.57), kind=kLoop, calls=%fused_computation.19 | loop fusion | flops 491520 | bytes 1966080 | tf_op jit(solution)/shard_map/concatenate | solution.py:91
  49.0 2.6 %copy.60 = bf16[16,128,240]{1,2,0:T(8,128)(2,1)} copy(bf16[16,128,240]{2,0,1:T(8,128)(2,1)} %pad_maximum_fusion) | data formatting | bytes 1966080 | tf_op jit(solution)/shard_map/concatenate | solution.py:91
  51.7 0.0 all-to-all-done.1
  51.7 4.3 %all-to-all-start = ((bf16[16,128,240]{1,2,0:T(8,128)(2,1)}), bf16[16,128,240]{1,2,0:T(8,128)(2,1)}, u32[]{:S(2)}, u32[]{:S(2)}) async-start(bf16[16,128,240]{1,2,0:T(8,128)(2,1)} %copy.60), calls=%async_computation | async-start | bytes 1966080 | tf_op jit(solution)/shard_map/all_to_all | solution.py:87
  56.0 4.1 %copy.63 = bf16[256,4096]{0,1:T(8,128)(2,1)} copy(bf16[256,4096]{1,0:T(8,128)(2,1)} %param.10) | data formatting | bytes 4194304 | tf_op args[4]
  60.1 4.1 %copy.64 = bf16[256,32,128]{2,0,1:T(8,128)(2,1)} copy(bf16[256,32,128]{0,2,1:T(8,128)(2,1)} %bitcast.48) | data formatting | bytes 4194304 | tf_op jit(solution)/shard_map/reshape | solution.py:66
  64.1 3.7 %gather_fusion.2 = bf16[30,256,128]{2,1,0:T(8,128)(2,1)} fusion(bf16[256,32,128]{2,0,1:T(8,128)(2,1)} %copy.64, s32[1024]{0:T(1024)S(1)} %pad_clamp_fusion), kind=kCustom, calls=%fused_computation.2 | custom fusion | bytes 3932280 | tf_op jit(solution)/shard_map/jit(_take)/gather | solution.py:67
  67.8 4.0 %copy.65 = bf16[256,30,128]{0,2,1:T(8,128)(2,1)} copy(bf16[256,30,128]{2,0,1:T(8,128)(2,1)} %bitcast.47) | data formatting | bytes 3932160 | tf_op jit(solution)/shard_map/jit(_take)/gather | solution.py:67
  71.8 6.0 %all-to-all-done = bf16[16,128,240]{1,2,0:T(8,128)(2,1)} async-done(((bf16[16,128,240]{1,2,0:T(8,128)(2,1)}), bf16[16,128,240]{1,2,0:T(8,128)(2,1)}, u32[]{:S(2)}, u32[]{:S(2)}) %all-to-all-start) | async-done | bytes 983072 | tf_op jit(solution)/shard_map/all_to_all | solution.py:87
  77.9 1.3 convert_reduce_fusion
  79.2 0.1 fusion.26
  79.3 0.1 copy.61
  79.4 23.7 %all-gather.1 = bf16[16,240,64]{1,2,0:T(8,128)(2,1)S(1)} all-gather(bf16[1,240,64]{1,2,0:T(8,128)(2,1)S(1)} %bitcast.59), channel_id=1, replica_groups=mesh['groups'=2,'dp'=16] {'dp'}, dimensions={0}, use_global_device_ids=true | all-gather | bytes 522240 | tf_op jit(solution)/shard_map/all_gather | solution.py:97
  103.2 0.3 copy.62
  103.4 1.6 %reshape.71 = bf16[3840,64]{0,1:T(8,128)(2,1)} reshape(bf16[16,240,64]{1,0,2:T(8,128)(2,1)S(1)} %copy.62) | data formatting | bytes 983040
  105.0 2.3 %fusion.6 = bf16[64,256]{1,0:T(8,128)(2,1)S(1)} fusion(f32[64,256]{1,0:T(8,128)S(1)} %reshape.31, bf16[3840,64]{0,1:T(8,128)(2,1)} %reshape.71, bf16[256,3840]{0,1:T(8,128)(2,1)} %bitcast.49), kind=kOutput, calls=%fused_computation.18 | convolution fusion | flops 125878272 | bytes 2555904 | tf_op jit(solution)/shard_map/dot_general | solution.py:99
  107.3 0.0 copy-done.1
  107.3 0.5 fusion.4
  107.8 0.9 copy.78
  108.8 1.7 %gather_fusion.3 = bf16[30,64,128]{2,1,0:T(8,128)(2,1)S(1)} fusion(bf16[64,32,128]{2,0,1:T(8,128)(2,1)} %bitcast.54, s32[1024]{0:T(1024)S(1)} %pad_clamp_fusion), kind=kCustom, calls=%fused_computation.3 | custom fusion | bytes 983160 | tf_op jit(solution)/shard_map/jit(_take)/gather | solution.py:67
  110.5 1.1 copy.68
  111.6 2.1 %reshape_reshape.11 = bf16[64,16,240]{2,1,0:T(8,128)(2,1)S(1)} reshape(bf16[64,30,128]{2,1,0:T(8,128)(2,1)} %copy.68) | data formatting | bytes 983040 | tf_op jit(solution)/shard_map/reshape;reshape | solution.py:84
  113.7 1.0 copy.69
  114.6 3.6 %all-to-all-start.2 = ((bf16[16,64,240]{2,1,0:T(8,128)(2,1)}), bf16[16,64,240]{2,1,0:T(8,128)(2,1)S(1)}, u32[]{:S(2)}, u32[]{:S(2)}) async-start(bf16[16,64,240]{2,1,0:T(8,128)(2,1)} %copy.69), calls=%async_computation.2 | async-start | bytes 1048576 | tf_op jit(solution)/shard_map/all_to_all | solution.py:87
  118.2 26.8 %all_gather.11 = bf16[64,4096]{1,0:T(8,128)(2,1)S(1)} all-gather(bf16[64,256]{1,0:T(8,128)(2,1)S(1)} %fusion.6), channel_id=1, replica_groups=mesh['groups'=2,'dp'=16] {'dp'}, dimensions={1}, use_global_device_ids=true | all-gather | bytes 557056 | tf_op jit(solution)/shard_map/all_gather | solution.py:103
  145.0 2.0 %convolution_convert_fusion = bf16[4096,240]{0,1:T(8,128)(2,1)} fusion(bf16[64,4096]{1,0:T(8,128)(2,1)S(1)} %all_gather.11, f32[128,240]{0,1:T(8,128)S(1)} %convert_reduce_fusion), kind=kOutput, calls=%fused_computation.4 | convolution fusion | flops 126904320 | bytes 2736128 | tf_op jit(solution)/shard_map/dot_general | solution.py:105
  147.0 0.0 all-to-all-done.2
  147.0 0.1 convert_reduce_fusion.1
  147.1 0.1 copy.70
  147.2 1.9 %fusion.1 = bf16[4096,240]{0,1:T(8,128)(2,1)} fusion(bf16[64,4096]{1,0:T(8,128)(2,1)S(1)} %reshape.69, f32[64,240]{0,1:T(8,128)S(1)} %copy.70, f32[128,240]{0,1:T(8,128)S(1)} %convert_reduce_fusion), kind=kOutput, calls=%fused_computation.8 | convolution fusion | flops 126904320 | bytes 2674688 | tf_op jit(solution)/shard_map/dot_general | solution.py:114
  149.1 2.0 %fusion = bf16[4096,240]{0,1:T(8,128)(2,1)} fusion(bf16[64,4096]{1,0:T(8,128)(2,1)S(1)} %reshape.69, f32[64,240]{0,1:T(8,128)S(1)} %copy.70, f32[128,240]{0,1:T(8,128)S(1)} %convert_reduce_fusion), kind=kOutput, calls=%fused_computation.7 | convolution fusion | flops 126965760 | bytes 2859008 | tf_op jit(solution)/shard_map/dot_general | solution.py:111
  (4 shorter events, 0.0 us)
Async XLA Ops:
  0.6 31.1 %copy-start = (bf16[256,4096]{1,0:T(8,128)(2,1)S(1)}, bf16[256,4096]{1,0:T(8,128)(2,1)}, u32[]{:S(2)}) copy-start(bf16[256,4096]{1,0:T(8,128)(2,1)} %param.8) | copy-start | bytes 6291460
  0.6 51.0 %all-to-all-start.1 = ((bf16[4,16,256]{2,0,1:T(4,128)(2,1)}), bf16[4,16,256]{2,0,1:T(4,128)(2,1)S(1)}, u32[]{:S(2)}, u32[]{:S(2)}) async-start(bf16[4,16,256]{2,0,1:T(4,128)(2,1)} %bitcast.61), calls=%async_computation.1 | async-start | bytes 65536 | tf_op jit(solution)/shard_map/all_to_all | solution.py:77
  31.8 1.5 copy-start.2
  51.7 26.2 %all-to-all-start = ((bf16[16,128,240]{1,2,0:T(8,128)(2,1)}), bf16[16,128,240]{1,2,0:T(8,128)(2,1)}, u32[]{:S(2)}, u32[]{:S(2)}) async-start(bf16[16,128,240]{1,2,0:T(8,128)(2,1)} %copy.60), calls=%async_computation | async-start | bytes 1966080 | tf_op jit(solution)/shard_map/all_to_all | solution.py:87
  105.0 2.3 %copy-start.1 = (bf16[256,4096]{1,0:T(8,128)(2,1)S(1)}, bf16[256,4096]{1,0:T(8,128)(2,1)}, u32[]{:S(2)}) copy-start(bf16[256,4096]{1,0:T(8,128)(2,1)} %param.10) | copy-start | bytes 6291460
  114.6 32.4 %all-to-all-start.2 = ((bf16[16,64,240]{2,1,0:T(8,128)(2,1)}), bf16[16,64,240]{2,1,0:T(8,128)(2,1)S(1)}, u32[]{:S(2)}, u32[]{:S(2)}) async-start(bf16[16,64,240]{2,1,0:T(8,128)(2,1)} %copy.69), calls=%async_computation.2 | async-start | bytes 1048576 | tf_op jit(solution)/shard_map/all_to_all | solution.py:87

commit v2 on v0

--- a/solution.py
+++ b/solution.py
@@ -1,6 +1,10 @@
+import functools
+
 import jax
 import jax.numpy as jnp
 from jax import lax
+from jax.experimental import pallas as pl
+from jax.experimental.pallas import tpu as pltpu
 from jax.sharding import PartitionSpec as P
 
 BLK = 128
@@ -14,7 +18,7 @@
     return (kept_blocks[:, None] * BLK + offsets[None, :]).reshape(-1)
 
 
-def body(tokens, target, w_gate, w_up, w_down_t, kept_blocks):
+def gathered_weights_body(tokens, target, w_gate, w_up, w_down_t, kept_blocks):
     channels = channel_index(kept_blocks)
     picked_gate = jnp.take(w_gate, channels, axis=1)
     picked_up = jnp.take(w_up, channels, axis=1)
@@ -61,6 +65,240 @@
     )
 
 
+def exchange_kernel(
+    n, held, kept, packed, wg_hbm, wu_hbm, wd_hbm, gate_out, up_out, hid_out, tok_all, res_all,
+    wg, wu, wd, packs, tok32, tgt32, tok16, full, sel, down32, down, act_out, act_in,
+    hid16, hid_in, res16, hg_out, hg_in, load_sem, send_sem, recv_sem,
+):
+    me = lax.axis_index("dp")
+    rows, features = tok16.shape
+    wide = hid16.shape[1]
+    kept_count = kept.shape[0]
+    mine = rows // n
+    bf16, f32 = jnp.bfloat16, jnp.float32
+
+    loads = [
+        pltpu.make_async_copy(src, dst, load_sem.at[i])
+        for i, (src, dst) in enumerate(((wg_hbm, wg), (wu_hbm, wu), (wd_hbm, wd)))
+    ]
+    for load in loads:
+        load.start()
+
+    barrier = pltpu.get_barrier_semaphore()
+
+    @pl.loop(1, n)
+    def _(k):
+        pl.semaphore_signal(
+            barrier, inc=1, device_id={"dp": lax.rem(me + k, n)},
+            device_id_type=pl.DeviceIdType.MESH,
+        )
+
+    pl.semaphore_wait(barrier, n - 1)
+
+    def remote(phase, k, src, dst):
+        return pltpu.make_async_remote_copy(
+            src_ref=src, dst_ref=dst, send_sem=send_sem.at[phase, k],
+            recv_sem=recv_sem.at[phase, k], device_id={"dp": lax.rem(me + k, n)},
+            device_id_type=pl.DeviceIdType.MESH,
+        )
+
+    def columns(index):
+        return pl.ds(pl.multiple_of(index * features, features), features)
+
+    def pack_copy(k):
+        return remote(0, k, packed.at[:, columns(lax.rem(me + k, n))], packs.at[me])
+
+    def act_copy(k):
+        return remote(1, k, act_out.at[lax.rem(me + k, n)], act_in.at[me])
+
+    def hid_copy(k):
+        return remote(2, k, hid16, hid_in.at[me])
+
+    def res_copy(k):
+        return remote(3, k, res16, res_all.at[:, columns(me)])
+
+    def hg_copy(k):
+        return remote(4, k, hg_out.at[lax.rem(me + k, n)], hg_in.at[me])
+
+    def tok_copy(k):
+        return remote(5, k, tok16, tok_all.at[:, columns(me)])
+
+    spare = wd.shape[1] // BLK - kept_count
+
+    def kept_block(ref, b):
+        shift = jnp.full((ref.shape[0], BLK), kept[b] - b, jnp.int32)
+        chosen = ref[:, b * BLK:(b + 1) * BLK].astype(f32)
+        for j in range(1, spare + 1):
+            other = ref[:, (b + j) * BLK:(b + j + 1) * BLK].astype(f32)
+            chosen = jnp.where(shift == j, other, chosen)
+        return chosen
+
+    def start_all(copy):
+        @pl.loop(1, n)
+        def _(k):
+            copy(k).start()
+
+    def receive_all(copy):
+        @pl.loop(1, n)
+        def _(k):
+            copy(k).wait_recv()
+
+    def sent_all(copy):
+        @pl.loop(1, n)
+        def _(k):
+            copy(k).wait_send()
+
+    start_all(pack_copy)
+    packs[me] = packed[:, columns(me)]
+    receive_all(pack_copy)
+    for s in range(n):
+        piece = packs[s].astype(f32)
+        tok32[s * mine:(s + 1) * mine, :] = piece[:mine]
+        tgt32[s * mine:(s + 1) * mine, :] = piece[mine:2 * mine]
+    tok16[...] = tok32[...].astype(bf16)
+
+    loads[0].wait()
+    loads[1].wait()
+    for half, weight in enumerate((wg, wu)):
+        here = pl.ds(half * rows, rows)
+        for c in range(0, weight.shape[1], 512):
+            full[here, c:c + 512] = jnp.dot(
+                tok16[...], weight[:, c:c + 512], preferred_element_type=f32
+            )
+    sel[:, kept_count * BLK:] = jnp.zeros((2 * rows, BLK), f32)
+    for b in range(kept_count):
+        sel[:, b * BLK:(b + 1) * BLK] = kept_block(full, b)
+    for p in range(n):
+        act_out[p] = sel[:, p * held:p * held + wide].astype(bf16)
+    start_all(act_copy)
+    act_in[me] = act_out[me]
+    start_all(tok_copy)
+    tok_all[:, columns(me)] = tok16[...]
+
+    loads[2].wait()
+    down32[:, kept_count * BLK:] = jnp.zeros((features, BLK), f32)
+    for b in range(kept_count):
+        down32[:, b * BLK:(b + 1) * BLK] = kept_block(wd, b)
+    for p in range(n):
+        down[p] = down32[:, p * held:p * held + wide].astype(bf16)
+
+    receive_all(act_copy)
+    both = act_in[0].astype(f32)
+    for s in range(1, n):
+        both = both + act_in[s].astype(f32)
+    gate_act, up_act = both[:rows], both[rows:]
+    sigmoid_gate = jax.nn.sigmoid(gate_act)
+    silu_gate = gate_act * sigmoid_gate
+    inside = lax.broadcasted_iota(jnp.int32, (rows, wide), 1) < held
+    hidden = jnp.where(inside, silu_gate * up_act, 0.0).astype(bf16)
+    hid16[...] = hidden
+    hid_out[...] = hidden
+    start_all(hid_copy)
+    hid_in[me] = hidden
+    receive_all(hid_copy)
+
+    output = jnp.zeros((rows, features), f32)
+    for s in range(n):
+        output = output + lax.dot_general(
+            hid_in[s], down[s], (((1,), (1,)), ((), ())), preferred_element_type=f32
+        )
+    residual = ((output - tgt32[...]) * (LOSS_SCALE / rows)).astype(bf16)
+    res16[...] = residual
+
+    @pl.loop(1, n)
+    def _(k):
+        p = lax.rem(me + k, n)
+        hg_out[p] = jnp.dot(res16[...], down[p], preferred_element_type=f32).astype(bf16)
+        hg_copy(k).start()
+
+    hg_in[me] = jnp.dot(res16[...], down[me], preferred_element_type=f32).astype(bf16)
+    start_all(res_copy)
+    res_all[:, columns(me)] = residual
+    receive_all(hg_copy)
+    hidden_grad = hg_in[0].astype(f32)
+    for s in range(1, n):
+        hidden_grad = hidden_grad + hg_in[s].astype(f32)
+    slope = sigmoid_gate * (1.0 + gate_act * (1.0 - sigmoid_gate))
+    gate_out[...] = (hidden_grad * up_act * slope).astype(bf16)
+    up_out[...] = (hidden_grad * silu_gate).astype(bf16)
+
+    receive_all(tok_copy)
+    receive_all(res_copy)
+    for copy in (pack_copy, act_copy, hid_copy, res_copy, hg_copy, tok_copy):
+        sent_all(copy)
+
+
+def resident_weights_body(tokens, target, w_gate, w_up, w_down_t, kept_blocks):
+    n = lax.axis_size("dp")
+    mine, width = tokens.shape
+    rows = mine * n
+    features, channels = w_gate.shape
+    kept_count = kept_blocks.shape[0]
+    held = kept_count * BLK // n
+    wide = -(-held // BLK) * BLK
+    pack_rows = -(-2 * mine // 16) * 16
+    filler = jnp.zeros((pack_rows - 2 * mine, width), tokens.dtype)
+    packed = jnp.concatenate([tokens, target, filler], axis=0)
+    bf16, f32 = jnp.bfloat16, jnp.float32
+    vmem = pl.BlockSpec(memory_space=pltpu.VMEM)
+    hbm = pl.BlockSpec(memory_space=pl.ANY)
+    small = jax.ShapeDtypeStruct((rows, wide), bf16)
+    large = jax.ShapeDtypeStruct((rows, width), bf16)
+    picked = kept_count * BLK + BLK
+    gate_grad, up_grad, hidden, tok_all, res_all = pl.pallas_call(
+        functools.partial(exchange_kernel, n, held),
+        out_shape=(small, small, small, large, large),
+        in_specs=[pl.BlockSpec(memory_space=pltpu.SMEM), vmem, hbm, hbm, hbm],
+        out_specs=(vmem,) * 5,
+        scratch_shapes=[
+            pltpu.VMEM((features, channels), bf16),
+            pltpu.VMEM((features, channels), bf16),
+            pltpu.VMEM((features, channels), bf16),
+            pltpu.VMEM((n, pack_rows, features), bf16),
+            pltpu.VMEM((rows, features), f32),
+            pltpu.VMEM((rows, features), f32),
+            pltpu.VMEM((rows, features), bf16),
+            pltpu.VMEM((2 * rows, channels), f32),
+            pltpu.VMEM((2 * rows, picked), f32),
+            pltpu.VMEM((features, picked), f32),
+            pltpu.VMEM((n, features, wide), bf16),
+            pltpu.VMEM((n, 2 * rows, wide), bf16),
+            pltpu.VMEM((n, 2 * rows, wide), bf16),
+            pltpu.VMEM((rows, wide), bf16),
+            pltpu.VMEM((n, rows, wide), bf16),
+            pltpu.VMEM((rows, features), bf16),
+            pltpu.VMEM((n, rows, wide), bf16),
+            pltpu.VMEM((n, rows, wide), bf16),
+            pltpu.SemaphoreType.DMA((3,)),
+            pltpu.SemaphoreType.DMA((6, n)),
+            pltpu.SemaphoreType.DMA((6, n)),
+        ],
+        compiler_params=pltpu.CompilerParams(
+            collective_id=0, has_side_effects=True, vmem_limit_bytes=44 * 1024 * 1024
+        ),
+    )(kept_blocks, packed, w_gate, w_up, w_down_t)
+
+    def over_tokens(left, right):
+        product = lax.dot_general(
+            left, right[:, :held], (((0,), (0,)), ((), ())), preferred_element_type=f32
+        )
+        return product.astype(bf16)
+
+    return (
+        over_tokens(tok_all, gate_grad),
+        over_tokens(tok_all, up_grad),
+        over_tokens(res_all, hidden),
+    )
+
+
+def body(tokens, target, w_gate, w_up, w_down_t, kept_blocks):
+    token_rows = tokens.shape[0] * lax.axis_size("dp")
+    few_tokens = token_rows < w_gate.shape[0]
+    few_dropped = w_gate.shape[1] // BLK - kept_blocks.shape[0] <= 4
+    chosen = resident_weights_body if few_tokens and few_dropped else gathered_weights_body
+    return chosen(tokens, target, w_gate, w_up, w_down_t, kept_blocks)
+
+
 def solution(mesh):
     placed = (
         P(("groups", "dp"), None),

time: 364 us -> 97.5 us (0.27)
  the two profiles are of different devices: /device:TPU:0 before, /device:TPU:29 now
where the time goes in v2:
time: 97.5 us; the launch traced here: 97.2 us
  Pallas kernels  84.2 us (86%)
  matrix products  5.94 us (6%)
  local copies, waits for them, and re-layouts  5.5 us (6%)
    pallas_call x1, Pallas kernels, resident_weights_body(): pl.pallas_call(functools.partial(exchange_kernel, n, held), out_shape=(sm...  84.2 us
    dot_general x3, matrix products, over_tokens(): lax.dot_general(left, right[:, :held], (((0,), (0,)), ((), ())), preferre...  5.94 us
    unnamed x8, local copies, waits for them, and re-layouts  5.42 us

profile of v2, /device:TPU:29, one launch (start us, length us, event | category | flops | bytes accessed | tf_op | source)
XLA Modules:
  0.0 97.2 jit_solution(4524716199661052742)
XLA Ops:
  0.6 0.1 pad.2.clone
  0.7 0.9 maximum_maximum_fusion.packed
  1.6 0.0 copy-start
  1.6 1.6 %copy-done = bf16[256,4096]{1,0:T(8,128)(2,1)S(1)} copy-done((bf16[256,4096]{1,0:T(8,128)(2,1)S(1)}, bf16[256,4096]{1,0:T(8,128)(2,1)}, u32[]{:S(2)}) %copy-start) | copy-done | bytes 2097176
  3.2 0.0 copy-start.1
  3.2 1.6 %copy-done.1 = bf16[256,4096]{1,0:T(8,128)(2,1)S(1)} copy-done((bf16[256,4096]{1,0:T(8,128)(2,1)S(1)}, bf16[256,4096]{1,0:T(8,128)(2,1)}, u32[]{:S(2)}) %copy-start.1) | copy-done | bytes 2097176
  4.8 0.0 copy-start.2
  4.8 1.6 %copy-done.2 = bf16[256,4096]{1,0:T(8,128)(2,1)S(1)} copy-done((bf16[256,4096]{1,0:T(8,128)(2,1)S(1)}, bf16[256,4096]{1,0:T(8,128)(2,1)}, u32[]{:S(2)}) %copy-start.2) | copy-done | bytes 2097176
  6.4 0.0 copy-start.3
  6.4 0.7 copy-done.3
  7.0 84.2 %shard_map.85 = (bf16[64,256]{1,0:T(8,128)(2,1)S(1)}, bf16[64,256]{1,0:T(8,128)(2,1)S(1)}, bf16[64,256]{1,0:T(8,128)(2,1)S(1)}, bf16[64,4096]{1,0:T(8,128)(2,1)S(1)}, bf16[64,4096]{1,0:T(8,128)(2,1)S(1)}) custom-call(s32[30]{0:T(128)S(1)} %copy-done.3, bf16[16,4096]{1,0:T(8,128)(2,1)S(1)} %maximum_maximum_fusion.packed, bf16[256,4096]{1,0:T(8,128)(2,1)S(1)} %copy-done, ...), custom_call_target="tpu_custom_call" | custom-call | tf_op jit(solution)/shard_map/pallas_call | solution.py:248
  91.2 2.0 %convolution_convert_fusion.2 = bf16[4096,240]{0,1:T(8,128)(2,1)} fusion(bf16[64,4096]{1,0:T(8,128)(2,1)S(1)} %get-tuple-element.8, bf16[64,256]{1,0:T(8,128)(2,1)S(1)} %get-tuple-element.9), kind=kOutput, calls=%fused_computation.2 | convolution fusion | flops 126812160 | bytes 2523136 | tf_op jit(solution)/shard_map/dot_general | solution.py:282
  93.2 2.0 %convolution_convert_fusion.1 = bf16[4096,240]{0,1:T(8,128)(2,1)} fusion(bf16[64,4096]{1,0:T(8,128)(2,1)S(1)} %get-tuple-element.8, bf16[64,256]{1,0:T(8,128)(2,1)S(1)} %get-tuple-element.10), kind=kOutput, calls=%fused_computation.1 | convolution fusion | flops 126812160 | bytes 2523136 | tf_op jit(solution)/shard_map/dot_general | solution.py:282
  95.2 2.0 %convolution_convert_fusion = bf16[4096,240]{0,1:T(8,128)(2,1)} fusion(bf16[64,4096]{1,0:T(8,128)(2,1)S(1)} %get-tuple-element.11, bf16[64,256]{1,0:T(8,128)(2,1)S(1)} %get-tuple-element.12), kind=kOutput, calls=%fused_computation | convolution fusion | flops 126812160 | bytes 2523136 | tf_op jit(solution)/shard_map/dot_general | solution.py:282
  (1 shorter events, 0.0 us)
Async XLA Ops:
  1.6 1.6 %copy-start = (bf16[256,4096]{1,0:T(8,128)(2,1)S(1)}, bf16[256,4096]{1,0:T(8,128)(2,1)}, u32[]{:S(2)}) copy-start(bf16[256,4096]{1,0:T(8,128)(2,1)} %wg_hbm.1) | copy-start | bytes 6291460
  3.2 1.6 %copy-start.1 = (bf16[256,4096]{1,0:T(8,128)(2,1)S(1)}, bf16[256,4096]{1,0:T(8,128)(2,1)}, u32[]{:S(2)}) copy-start(bf16[256,4096]{1,0:T(8,128)(2,1)} %wu_hbm.1) | copy-start | bytes 6291460
  4.8 1.6 %copy-start.2 = (bf16[256,4096]{1,0:T(8,128)(2,1)S(1)}, bf16[256,4096]{1,0:T(8,128)(2,1)}, u32[]{:S(2)}) copy-start(bf16[256,4096]{1,0:T(8,128)(2,1)} %wd_hbm.1) | copy-start | bytes 6291460
  6.4 0.7 copy-start.3

commit v3 on v2

--- a/solution.py
+++ b/solution.py
@@ -95,13 +95,58 @@
 
     pl.semaphore_wait(barrier, n - 1)
 
-    def remote(phase, k, src, dst):
+    def remote(phase, k, src, dst, to=None):
         return pltpu.make_async_remote_copy(
             src_ref=src, dst_ref=dst, send_sem=send_sem.at[phase, k],
-            recv_sem=recv_sem.at[phase, k], device_id={"dp": lax.rem(me + k, n)},
+            recv_sem=recv_sem.at[phase, k],
+            device_id={"dp": lax.rem(me + k, n) if to is None else to},
             device_id_type=pl.DeviceIdType.MESH,
         )
 
+    chips = n // 2
+    sibling = me + 1 - 2 * lax.rem(me, 2)
+
+    def gather_copies(phase, own, slot):
+        def across(k):
+            return remote(phase, k, own, slot(me), lax.rem(me + 2 * k, n))
+
+        def beside():
+            return remote(phase, 0, own, slot(me), sibling)
+
+        def onward(k):
+            held_slot = slot(lax.rem(me + n - 2 * k, n))
+            return remote(phase, chips + k, held_slot, held_slot, sibling)
+
+        def start():
+            @pl.loop(1, chips)
+            def _(k):
+                across(k).start()
+
+            beside().start()
+
+        def forward():
+            @pl.loop(1, chips)
+            def _(k):
+                across(k).wait_recv()
+                onward(k).start()
+
+        def finish():
+            beside().wait_recv()
+
+            @pl.loop(1, chips)
+            def _(k):
+                onward(k).wait_recv()
+
+        def sent():
+            beside().wait_send()
+
+            @pl.loop(1, chips)
+            def _(k):
+                across(k).wait_send()
+                onward(k).wait_send()
+
+        return start, forward, finish, sent
+
     def columns(index):
         return pl.ds(pl.multiple_of(index * features, features), features)
 
@@ -111,17 +156,18 @@
     def act_copy(k):
         return remote(1, k, act_out.at[lax.rem(me + k, n)], act_in.at[me])
 
-    def hid_copy(k):
-        return remote(2, k, hid16, hid_in.at[me])
-
-    def res_copy(k):
-        return remote(3, k, res16, res_all.at[:, columns(me)])
-
     def hg_copy(k):
         return remote(4, k, hg_out.at[lax.rem(me + k, n)], hg_in.at[me])
 
-    def tok_copy(k):
-        return remote(5, k, tok16, tok_all.at[:, columns(me)])
+    hid_start, hid_forward, hid_finish, hid_sent = gather_copies(
+        2, hid16, lambda i: hid_in.at[i]
+    )
+    res_start, res_forward, res_finish, res_sent = gather_copies(
+        3, res16, lambda i: res_all.at[:, columns(i)]
+    )
+    tok_start, tok_forward, tok_finish, tok_sent = gather_copies(
+        5, tok16, lambda i: tok_all.at[:, columns(i)]
+    )
 
     spare = wd.shape[1] // BLK - kept_count
 
@@ -156,6 +202,7 @@
         tok32[s * mine:(s + 1) * mine, :] = piece[:mine]
         tgt32[s * mine:(s + 1) * mine, :] = piece[mine:2 * mine]
     tok16[...] = tok32[...].astype(bf16)
+    tok_start()
 
     loads[0].wait()
     loads[1].wait()
@@ -172,7 +219,6 @@
         act_out[p] = sel[:, p * held:p * held + wide].astype(bf16)
     start_all(act_copy)
     act_in[me] = act_out[me]
-    start_all(tok_copy)
     tok_all[:, columns(me)] = tok16[...]
 
     loads[2].wait()
@@ -182,6 +228,7 @@
     for p in range(n):
         down[p] = down32[:, p * held:p * held + wide].astype(bf16)
 
+    tok_forward()
     receive_all(act_copy)
     both = act_in[0].astype(f32)
     for s in range(1, n):
@@ -193,9 +240,10 @@
     hidden = jnp.where(inside, silu_gate * up_act, 0.0).astype(bf16)
     hid16[...] = hidden
     hid_out[...] = hidden
-    start_all(hid_copy)
+    hid_start()
     hid_in[me] = hidden
-    receive_all(hid_copy)
+    hid_forward()
+    hid_finish()
 
     output = jnp.zeros((rows, features), f32)
     for s in range(n):
@@ -212,8 +260,9 @@
         hg_copy(k).start()
 
     hg_in[me] = jnp.dot(res16[...], down[me], preferred_element_type=f32).astype(bf16)
-    start_all(res_copy)
+    res_start()
     res_all[:, columns(me)] = residual
+    res_forward()
     receive_all(hg_copy)
     hidden_grad = hg_in[0].astype(f32)
     for s in range(1, n):
@@ -222,10 +271,12 @@
     gate_out[...] = (hidden_grad * up_act * slope).astype(bf16)
     up_out[...] = (hidden_grad * silu_gate).astype(bf16)
 
-    receive_all(tok_copy)
-    receive_all(res_copy)
-    for copy in (pack_copy, act_copy, hid_copy, res_copy, hg_copy, tok_copy):
+    tok_finish()
+    res_finish()
+    for copy in (pack_copy, act_copy, hg_copy):
         sent_all(copy)
+    for sent in (tok_sent, hid_sent, res_sent):
+        sent()
 
 
 def resident_weights_body(tokens, target, w_gate, w_up, w_down_t, kept_blocks):
@@ -241,7 +292,7 @@
     packed = jnp.concatenate([tokens, target, filler], axis=0)
     bf16, f32 = jnp.bfloat16, jnp.float32
     vmem = pl.BlockSpec(memory_space=pltpu.VMEM)
-    hbm = pl.BlockSpec(memory_space=pl.ANY)
+    hbm = pl.BlockSpec(memory_space=pltpu.HBM)
     small = jax.ShapeDtypeStruct((rows, wide), bf16)
     large = jax.ShapeDtypeStruct((rows, width), bf16)
     picked = kept_count * BLK + BLK
@@ -274,7 +325,7 @@
             pltpu.SemaphoreType.DMA((6, n)),
         ],
         compiler_params=pltpu.CompilerParams(
-            collective_id=0, has_side_effects=True, vmem_limit_bytes=44 * 1024 * 1024
+            collective_id=0, has_side_effects=True, vmem_limit_bytes=58 * 1024 * 1024
         ),
     )(kept_blocks, packed, w_gate, w_up, w_down_t)
 
@@ -295,7 +346,9 @@
     token_rows = tokens.shape[0] * lax.axis_size("dp")
     few_tokens = token_rows < w_gate.shape[0]
     few_dropped = w_gate.shape[1] // BLK - kept_blocks.shape[0] <= 4
-    chosen = resident_weights_body if few_tokens and few_dropped else gathered_weights_body
+    paired = lax.axis_size("dp") % 2 == 0
+    resident = few_tokens and few_dropped and paired
+    chosen = resident_weights_body if resident else gathered_weights_body
     return chosen(tokens, target, w_gate, w_up, w_down_t, kept_blocks)
 
 

time: 97.5 us -> 82.3 us (0.84)
  the two profiles are of different devices: /device:TPU:29 before, /device:TPU:0 now
where the time goes in v3:
time: 82.3 us; the launch traced here: 81.3 us
  Pallas kernels  72 us (87%)
  matrix products  7.07 us (9%)
  other arithmetic  1.51 us (2%)
    pallas_call x1, Pallas kernels, resident_weights_body(): pl.pallas_call(functools.partial(exchange_kernel, n, held), out_shape=(sm...  72 us
    dot_general x3, matrix products, over_tokens(): lax.dot_general(left, right[:, :held], (((0,), (0,)), ((), ())), preferre...  7.07 us

profile of v3, /device:TPU:0, one launch (start us, length us, event | category | flops | bytes accessed | tf_op | source)
XLA Modules:
  0.0 81.3 jit_solution(17049834582071244306)
XLA Ops:
  0.6 0.1 pad.2.clone
  0.7 1.5 %maximum_maximum_fusion.packed = bf16[16,4096]{1,0:T(8,128)(2,1)} fusion(bf16[4,4096]{1,0:T(4,128)(2,1)} %param.7, bf16[4,4096]{1,0:T(4,128)(2,1)} %param.6, bf16[16]{0:T(256)(128)(2,1)S(1)} %pad.2.clone), kind=kLoop, calls=%fused_computation.3 | loop fusion | flops 393216 | bytes 196640 | tf_op jit(solution)/shard_map/concatenate | solution.py:292
  2.2 72.0 %shard_map.85 = (bf16[64,256]{1,0:T(8,128)(2,1)}, bf16[64,256]{1,0:T(8,128)(2,1)}, bf16[64,256]{1,0:T(8,128)(2,1)}, bf16[64,4096]{1,0:T(8,128)(2,1)}, bf16[64,4096]{1,0:T(8,128)(2,1)}) custom-call(s32[30]{0:T(128)} %kept.1, bf16[16,4096]{1,0:T(8,128)(2,1)} %maximum_maximum_fusion.packed, bf16[256,4096]{1,0:T(8,128)(2,1)} %wg_hbm.1, ...), custom_call_target="tpu_custom_call" | custom-call | tf_op jit(solution)/shard_map/pallas_call | solution.py:299
  74.2 0.0 copy-start
  74.2 0.0 copy-start.3
  74.2 0.0 copy-start.1
  74.2 0.0 copy-start.2
  74.3 3.1 %convolution_convert_fusion.2 = bf16[4096,240]{0,1:T(8,128)(2,1)} fusion(bf16[64,4096]{1,0:T(8,128)(2,1)} %get-tuple-element.8, bf16[64,256]{1,0:T(8,128)(2,1)} %get-tuple-element.9), kind=kOutput, calls=%fused_computation.2 | convolution fusion | flops 126812160 | bytes 2523136 | tf_op jit(solution)/shard_map/dot_general | solution.py:333
  77.4 0.0 copy-done
  77.4 0.0 copy-done.3
  77.4 2.0 %convolution_convert_fusion.1 = bf16[4096,240]{0,1:T(8,128)(2,1)} fusion(bf16[64,4096]{1,0:T(8,128)(2,1)S(1)} %copy-done, bf16[64,256]{1,0:T(8,128)(2,1)S(1)} %copy-done.3), kind=kOutput, calls=%fused_computation.1 | convolution fusion | flops 126812160 | bytes 2523136 | tf_op jit(solution)/shard_map/dot_general | solution.py:333
  79.4 0.0 copy-done.1
  79.4 0.0 copy-done.2
  79.4 2.0 %convolution_convert_fusion = bf16[4096,240]{0,1:T(8,128)(2,1)} fusion(bf16[64,4096]{1,0:T(8,128)(2,1)S(1)} %copy-done.1, bf16[64,256]{1,0:T(8,128)(2,1)S(1)} %copy-done.2), kind=kOutput, calls=%fused_computation | convolution fusion | flops 126812160 | bytes 2523136 | tf_op jit(solution)/shard_map/dot_general | solution.py:333
  (1 shorter events, 0.0 us)
Async XLA Ops:
  74.2 3.1 %copy-start = (bf16[64,4096]{1,0:T(8,128)(2,1)S(1)}, bf16[64,4096]{1,0:T(8,128)(2,1)}, u32[]{:S(2)}) copy-start(bf16[64,4096]{1,0:T(8,128)(2,1)} %get-tuple-element.8) | copy-start | bytes 1572868
  74.2 3.1 %copy-start.3 = (bf16[64,256]{1,0:T(8,128)(2,1)S(1)}, bf16[64,256]{1,0:T(8,128)(2,1)}, u32[]{:S(2)}) copy-start(bf16[64,256]{1,0:T(8,128)(2,1)} %get-tuple-element.10) | copy-start | bytes 98308
  74.2 5.1 %copy-start.1 = (bf16[64,4096]{1,0:T(8,128)(2,1)S(1)}, bf16[64,4096]{1,0:T(8,128)(2,1)}, u32[]{:S(2)}) copy-start(bf16[64,4096]{1,0:T(8,128)(2,1)} %get-tuple-element.11) | copy-start | bytes 1572868
  74.2 5.1 %copy-start.2 = (bf16[64,256]{1,0:T(8,128)(2,1)S(1)}, bf16[64,256]{1,0:T(8,128)(2,1)}, u32[]{:S(2)}) copy-start(bf16[64,256]{1,0:T(8,128)(2,1)} %get-tuple-element.12) | copy-start | bytes 98308

commit v4 on v3

--- a/solution.py
+++ b/solution.py
@@ -67,8 +67,8 @@
 
 def exchange_kernel(
     n, held, kept, packed, wg_hbm, wu_hbm, wd_hbm, gate_out, up_out, hid_out, tok_all, res_all,
-    wg, wu, wd, packs, tok32, tgt32, tok16, full, sel, down32, down, act_out, act_in,
-    hid16, hid_in, res16, hg_out, hg_in, load_sem, send_sem, recv_sem,
+    wg, wu, wd, packs, tok32, tgt32, tok16, full, sel, down32, down,
+    act_out, act_pair, act_sum, act_in, hid16, hid_in, res16, hg_out, hg_pair, hg_sum, hg_in, load_sem, send_sem, recv_sem,
 ):
     me = lax.axis_index("dp")
     rows, features = tok16.shape
@@ -153,12 +153,58 @@
     def pack_copy(k):
         return remote(0, k, packed.at[:, columns(lax.rem(me + k, n))], packs.at[me])
 
-    def act_copy(k):
-        return remote(1, k, act_out.at[lax.rem(me + k, n)], act_in.at[me])
-
-    def hg_copy(k):
-        return remote(4, k, hg_out.at[lax.rem(me + k, n)], hg_in.at[me])
-
+    core = lax.rem(me, 2)
+    chip = lax.div(me, 2)
+
+    def sum_copies(phase, out, pair, total, landed):
+        def there(k):
+            return lax.rem(chip + k, chips)
+
+        def beside(k):
+            j = there(k)
+            return remote(phase, k, out.at[2 * j + 1 - core], pair.at[j], sibling)
+
+        def across(k):
+            j = there(k)
+            return remote(phase, chips + k, total.at[j], landed.at[chip], 2 * j + core)
+
+        def combine():
+            @pl.loop(1, chips)
+            def _(k):
+                j = there(k)
+                beside(k).wait_recv()
+                total[j] = (out[2 * j + core] + pair[j]).astype(bf16)
+                across(k).start()
+
+            beside(0).wait_recv()
+            landed[chip] = (out[me] + pair[chip]).astype(bf16)
+
+        def finish():
+            @pl.loop(1, chips)
+            def _(k):
+                across(k).wait_recv()
+
+            result = landed[0].astype(f32)
+            for s in range(1, chips):
+                result = result + landed[s].astype(f32)
+            return result
+
+        def sent():
+            beside(0).wait_send()
+
+            @pl.loop(1, chips)
+            def _(k):
+                beside(k).wait_send()
+                across(k).wait_send()
+
+        return there, beside, combine, finish, sent
+
+    _, act_beside, act_combine, act_finish, act_sent = sum_copies(
+        1, act_out, act_pair, act_sum, act_in
+    )
+    hg_there, hg_beside, hg_combine, hg_finish, hg_sent = sum_copies(
+        4, hg_out, hg_pair, hg_sum, hg_in
+    )
     hid_start, hid_forward, hid_finish, hid_sent = gather_copies(
         2, hid16, lambda i: hid_in.at[i]
     )
@@ -216,9 +262,14 @@
     for b in range(kept_count):
         sel[:, b * BLK:(b + 1) * BLK] = kept_block(full, b)
     for p in range(n):
-        act_out[p] = sel[:, p * held:p * held + wide].astype(bf16)
-    start_all(act_copy)
-    act_in[me] = act_out[me]
+        act_out[p] = sel[:, p * held:p * held + wide]
+
+    @pl.loop(1, chips)
+    def _(k):
+        act_beside(k).start()
+
+    act_beside(0).start()
+    act_combine()
     tok_all[:, columns(me)] = tok16[...]
 
     loads[2].wait()
@@ -229,10 +280,7 @@
         down[p] = down32[:, p * held:p * held + wide].astype(bf16)
 
     tok_forward()
-    receive_all(act_copy)
-    both = act_in[0].astype(f32)
-    for s in range(1, n):
-        both = both + act_in[s].astype(f32)
+    both = act_finish()
     gate_act, up_act = both[:rows], both[rows:]
     sigmoid_gate = jax.nn.sigmoid(gate_act)
     silu_gate = gate_act * sigmoid_gate
@@ -253,29 +301,32 @@
     residual = ((output - tgt32[...]) * (LOSS_SCALE / rows)).astype(bf16)
     res16[...] = residual
 
-    @pl.loop(1, n)
+    def hg_piece(p):
+        hg_out[p] = jnp.dot(res16[...], down[p], preferred_element_type=f32)
+
+    @pl.loop(1, chips + 1)
+    def _(step):
+        k = lax.rem(step, chips)
+        hg_piece(2 * hg_there(k) + 1 - core)
+        hg_beside(k).start()
+
+    @pl.loop(0, chips)
     def _(k):
-        p = lax.rem(me + k, n)
-        hg_out[p] = jnp.dot(res16[...], down[p], preferred_element_type=f32).astype(bf16)
-        hg_copy(k).start()
-
-    hg_in[me] = jnp.dot(res16[...], down[me], preferred_element_type=f32).astype(bf16)
+        hg_piece(2 * hg_there(k) + core)
+
+    hg_combine()
     res_start()
     res_all[:, columns(me)] = residual
     res_forward()
-    receive_all(hg_copy)
-    hidden_grad = hg_in[0].astype(f32)
-    for s in range(1, n):
-        hidden_grad = hidden_grad + hg_in[s].astype(f32)
+    hidden_grad = hg_finish()
     slope = sigmoid_gate * (1.0 + gate_act * (1.0 - sigmoid_gate))
     gate_out[...] = (hidden_grad * up_act * slope).astype(bf16)
     up_out[...] = (hidden_grad * silu_gate).astype(bf16)
 
     tok_finish()
     res_finish()
-    for copy in (pack_copy, act_copy, hg_copy):
-        sent_all(copy)
-    for sent in (tok_sent, hid_sent, res_sent):
+    sent_all(pack_copy)
+    for sent in (act_sent, hg_sent, tok_sent, hid_sent, res_sent):
         sent()
 
 
@@ -313,13 +364,17 @@
             pltpu.VMEM((2 * rows, picked), f32),
             pltpu.VMEM((features, picked), f32),
             pltpu.VMEM((n, features, wide), bf16),
-            pltpu.VMEM((n, 2 * rows, wide), bf16),
-            pltpu.VMEM((n, 2 * rows, wide), bf16),
+            pltpu.VMEM((n, 2 * rows, wide), f32),
+            pltpu.VMEM((n // 2, 2 * rows, wide), f32),
+            pltpu.VMEM((n // 2, 2 * rows, wide), bf16),
+            pltpu.VMEM((n // 2, 2 * rows, wide), bf16),
             pltpu.VMEM((rows, wide), bf16),
             pltpu.VMEM((n, rows, wide), bf16),
             pltpu.VMEM((rows, features), bf16),
-            pltpu.VMEM((n, rows, wide), bf16),
-            pltpu.VMEM((n, rows, wide), bf16),
+            pltpu.VMEM((n, rows, wide), f32),
+            pltpu.VMEM((n // 2, rows, wide), f32),
+            pltpu.VMEM((n // 2, rows, wide), bf16),
+            pltpu.VMEM((n // 2, rows, wide), bf16),
             pltpu.SemaphoreType.DMA((3,)),
             pltpu.SemaphoreType.DMA((6, n)),
             pltpu.SemaphoreType.DMA((6, n)),

time: 82.3 us -> 66.2 us (0.80)
  Pallas kernels: 72 us -> 56.6 us
    pallas_call x1, Pallas kernels: 72 us -> 56.6 us  [resident_weights_body(): pl.pallas_call(functools.partial(exchange_kernel, n, held), out_shape=(sm...]
where the time goes in v4:
time: 66.2 us; the launch traced here: 66 us
  Pallas kernels  56.6 us (85%)
  matrix products  7.07 us (11%)
  other arithmetic  1.51 us (2%)
  between operations  0.68 us (1%)
    pallas_call x1, Pallas kernels, resident_weights_body(): pl.pallas_call(functools.partial(exchange_kernel, n, held), out_shape=(sm...  56.6 us
    dot_general x3, matrix products, over_tokens(): lax.dot_general(left, right[:, :held], (((0,), (0,)), ((), ())), preferre...  7.07 us
    concatenate x1, other arithmetic, resident_weights_body(): packed = jnp.concatenate([tokens, target, filler], axis=0)  1.51 us

profile of v4, /device:TPU:0, one launch (start us, length us, event | category | flops | bytes accessed | tf_op | source)
XLA Modules:
  0.0 66.0 jit_solution(17789977654925764748)
XLA Ops:
  0.6 0.1 pad.2.clone
  0.7 1.5 %maximum_maximum_fusion.packed = bf16[16,4096]{1,0:T(8,128)(2,1)} fusion(bf16[4,4096]{1,0:T(4,128)(2,1)} %param.7, bf16[4,4096]{1,0:T(4,128)(2,1)} %param.6, bf16[16]{0:T(256)(128)(2,1)S(1)} %pad.2.clone), kind=kLoop, calls=%fused_computation.3 | loop fusion | flops 393216 | bytes 196640 | tf_op jit(solution)/shard_map/concatenate | solution.py:343
  2.2 56.6 %shard_map.85 = (bf16[64,256]{1,0:T(8,128)(2,1)}, bf16[64,256]{1,0:T(8,128)(2,1)}, bf16[64,256]{1,0:T(8,128)(2,1)}, bf16[64,4096]{1,0:T(8,128)(2,1)}, bf16[64,4096]{1,0:T(8,128)(2,1)}) custom-call(s32[30]{0:T(128)} %kept.1, bf16[16,4096]{1,0:T(8,128)(2,1)} %maximum_maximum_fusion.packed, bf16[256,4096]{1,0:T(8,128)(2,1)} %wg_hbm.1, ...), custom_call_target="tpu_custom_call" | custom-call | tf_op jit(solution)/shard_map/pallas_call | solution.py:350
  58.9 0.0 copy-start
  58.9 0.0 copy-start.3
  58.9 0.0 copy-start.1
  58.9 0.0 copy-start.2
  58.9 3.1 %convolution_convert_fusion.2 = bf16[4096,240]{0,1:T(8,128)(2,1)} fusion(bf16[64,4096]{1,0:T(8,128)(2,1)} %get-tuple-element.8, bf16[64,256]{1,0:T(8,128)(2,1)} %get-tuple-element.9), kind=kOutput, calls=%fused_computation.2 | convolution fusion | flops 126812160 | bytes 2523136 | tf_op jit(solution)/shard_map/dot_general | solution.py:388
  62.0 0.0 copy-done
  62.0 0.0 copy-done.3
  62.0 2.0 %convolution_convert_fusion.1 = bf16[4096,240]{0,1:T(8,128)(2,1)} fusion(bf16[64,4096]{1,0:T(8,128)(2,1)S(1)} %copy-done, bf16[64,256]{1,0:T(8,128)(2,1)S(1)} %copy-done.3), kind=kOutput, calls=%fused_computation.1 | convolution fusion | flops 126812160 | bytes 2523136 | tf_op jit(solution)/shard_map/dot_general | solution.py:388
  64.0 0.0 copy-done.1
  64.0 0.0 copy-done.2
  64.0 2.0 %convolution_convert_fusion = bf16[4096,240]{0,1:T(8,128)(2,1)} fusion(bf16[64,4096]{1,0:T(8,128)(2,1)S(1)} %copy-done.1, bf16[64,256]{1,0:T(8,128)(2,1)S(1)} %copy-done.2), kind=kOutput, calls=%fused_computation | convolution fusion | flops 126812160 | bytes 2523136 | tf_op jit(solution)/shard_map/dot_general | solution.py:388
  (1 shorter events, 0.0 us)
Async XLA Ops:
  58.9 3.1 %copy-start = (bf16[64,4096]{1,0:T(8,128)(2,1)S(1)}, bf16[64,4096]{1,0:T(8,128)(2,1)}, u32[]{:S(2)}) copy-start(bf16[64,4096]{1,0:T(8,128)(2,1)} %get-tuple-element.8) | copy-start | bytes 1572868
  58.9 3.1 %copy-start.3 = (bf16[64,256]{1,0:T(8,128)(2,1)S(1)}, bf16[64,256]{1,0:T(8,128)(2,1)}, u32[]{:S(2)}) copy-start(bf16[64,256]{1,0:T(8,128)(2,1)} %get-tuple-element.10) | copy-start | bytes 98308
  58.9 5.1 %copy-start.1 = (bf16[64,4096]{1,0:T(8,128)(2,1)S(1)}, bf16[64,4096]{1,0:T(8,128)(2,1)}, u32[]{:S(2)}) copy-start(bf16[64,4096]{1,0:T(8,128)(2,1)} %get-tuple-element.11) | copy-start | bytes 1572868
  58.9 5.1 %copy-start.2 = (bf16[64,256]{1,0:T(8,128)(2,1)S(1)}, bf16[64,256]{1,0:T(8,128)(2,1)}, u32[]{:S(2)}) copy-start(bf16[64,256]{1,0:T(8,128)(2,1)} %get-tuple-element.12) | copy-start | bytes 98308

commit v5 on v4

--- a/solution.py
+++ b/solution.py
@@ -124,18 +124,21 @@
 
             beside().start()
 
-        def forward():
+        def forward(use=lambda i: None):
             @pl.loop(1, chips)
             def _(k):
                 across(k).wait_recv()
                 onward(k).start()
-
-        def finish():
+                use(lax.rem(me + n - 2 * k, n))
+
+        def finish(use=lambda i: None):
             beside().wait_recv()
+            use(sibling)
 
             @pl.loop(1, chips)
             def _(k):
                 onward(k).wait_recv()
+                use(lax.rem(sibling + n - 2 * k, n))
 
         def sent():
             beside().wait_send()
@@ -264,11 +267,10 @@
     for p in range(n):
         act_out[p] = sel[:, p * held:p * held + wide]
 
-    @pl.loop(1, chips)
-    def _(k):
-        act_beside(k).start()
-
-    act_beside(0).start()
+        @pl.when(core != p % 2)
+        def _(p=p):
+            act_beside(lax.rem(p // 2 + chips - chip, chips)).start()
+
     act_combine()
     tok_all[:, columns(me)] = tok16[...]
 
@@ -290,8 +292,278 @@
     hid_out[...] = hidden
     hid_start()
     hid_in[me] = hidden
-    hid_forward()
-    hid_finish()
+    tok32[...] = jnp.zeros((rows, features), f32)
+
+    def add_output(s):
+        tok32[...] += lax.dot_general(
+            hid_in[s], down[s], (((1,), (1,)), ((), ())), preferred_element_type=f32
+        )
+
+    add_output(me)
+    hid_forward(add_output)
+    hid_finish(add_output)
+
+    output = tok32[...]
+    residual = ((output_rows - target.astype(jnp.float32)) * scale).astype(jnp.bfloat16)
+    residual_all = lax.all_gather(residual, "dp", axis=0, tiled=True)
+    grad_down = lax.dot_general(
+        residual_all, hidden, (((0,), (0,)), ((), ())), preferred_element_type=jnp.float32
+    )
+    hidden_grad = jnp.dot(residual_all, student_down, preferred_element_type=jnp.float32)
+    slope = sigmoid_gate * (1.0 + gate_act * (1.0 - sigmoid_gate))
+    gate_grad = (hidden_grad * up_act * slope).astype(jnp.bfloat16)
+    up_grad = (hidden_grad * silu_gate).astype(jnp.bfloat16)
+    grad_gate = lax.dot_general(
+        gathered, gate_grad, (((0,), (0,)), ((), ())), preferred_element_type=jnp.float32
+    )
+    grad_up = lax.dot_general(
+        gathered, up_grad, (((0,), (0,)), ((), ())), preferred_element_type=jnp.float32
+    )
+    return (
+        grad_gate.astype(jnp.bfloat16),
+        grad_up.astype(jnp.bfloat16),
+        grad_down.astype(jnp.bfloat16),
+    )
+
+
+def exchange_kernel(
+    n, held, kept, packed, wg_hbm, wu_hbm, wd_hbm, gate_out, up_out, hid_out, tok_all, res_all,
+    wg, wu, wd, packs, tok32, tgt32, tok16, full, sel, down32, down,
+    act_out, act_pair, act_sum, act_in, hid16, hid_in, res16, hg_out, hg_pair, hg_sum, hg_in, load_sem, send_sem, recv_sem,
+):
+    me = lax.axis_index("dp")
+    rows, features = tok16.shape
+    wide = hid16.shape[1]
+    kept_count = kept.shape[0]
+    mine = rows // n
+    bf16, f32 = jnp.bfloat16, jnp.float32
+
+    loads = [
+        pltpu.make_async_copy(src, dst, load_sem.at[i])
+        for i, (src, dst) in enumerate(((wg_hbm, wg), (wu_hbm, wu), (wd_hbm, wd)))
+    ]
+    for load in loads:
+        load.start()
+
+    barrier = pltpu.get_barrier_semaphore()
+
+    @pl.loop(1, n)
+    def _(k):
+        pl.semaphore_signal(
+            barrier, inc=1, device_id={"dp": lax.rem(me + k, n)},
+            device_id_type=pl.DeviceIdType.MESH,
+        )
+
+    pl.semaphore_wait(barrier, n - 1)
+
+    def remote(phase, k, src, dst, to=None):
+        return pltpu.make_async_remote_copy(
+            src_ref=src, dst_ref=dst, send_sem=send_sem.at[phase, k],
+            recv_sem=recv_sem.at[phase, k],
+            device_id={"dp": lax.rem(me + k, n) if to is None else to},
+            device_id_type=pl.DeviceIdType.MESH,
+        )
+
+    chips = n // 2
+    sibling = me + 1 - 2 * lax.rem(me, 2)
+
+    def gather_copies(phase, own, slot):
+        def across(k):
+            return remote(phase, k, own, slot(me), lax.rem(me + 2 * k, n))
+
+        def beside():
+            return remote(phase, 0, own, slot(me), sibling)
+
+        def onward(k):
+            held_slot = slot(lax.rem(me + n - 2 * k, n))
+            return remote(phase, chips + k, held_slot, held_slot, sibling)
+
+        def start():
+            @pl.loop(1, chips)
+            def _(k):
+                across(k).start()
+
+            beside().start()
+
+        def forward(use=lambda i: None):
+            @pl.loop(1, chips)
+            def _(k):
+                across(k).wait_recv()
+                onward(k).start()
+                use(lax.rem(me + n - 2 * k, n))
+
+        def finish(use=lambda i: None):
+            beside().wait_recv()
+            use(sibling)
+
+            @pl.loop(1, chips)
+            def _(k):
+                onward(k).wait_recv()
+                use(lax.rem(sibling + n - 2 * k, n))
+
+        def sent():
+            beside().wait_send()
+
+            @pl.loop(1, chips)
+            def _(k):
+                across(k).wait_send()
+                onward(k).wait_send()
+
+        return start, forward, finish, sent
+
+    def columns(index):
+        return pl.ds(pl.multiple_of(index * features, features), features)
+
+    def pack_copy(k):
+        return remote(0, k, packed.at[:, columns(lax.rem(me + k, n))], packs.at[me])
+
+    core = lax.rem(me, 2)
+    chip = lax.div(me, 2)
+
+    def sum_copies(phase, out, pair, total, landed):
+        def there(k):
+            return lax.rem(chip + k, chips)
+
+        def beside(k):
+            j = there(k)
+            return remote(phase, k, out.at[2 * j + 1 - core], pair.at[j], sibling)
+
+        def across(k):
+            j = there(k)
+            return remote(phase, chips + k, total.at[j], landed.at[chip], 2 * j + core)
+
+        def combine():
+            @pl.loop(1, chips)
+            def _(k):
+                j = there(k)
+                beside(k).wait_recv()
+                total[j] = (out[2 * j + core] + pair[j]).astype(bf16)
+                across(k).start()
+
+            beside(0).wait_recv()
+            landed[chip] = (out[me] + pair[chip]).astype(bf16)
+
+        def finish():
+            @pl.loop(1, chips)
+            def _(k):
+                across(k).wait_recv()
+
+            result = landed[0].astype(f32)
+            for s in range(1, chips):
+                result = result + landed[s].astype(f32)
+            return result
+
+        def sent():
+            beside(0).wait_send()
+
+            @pl.loop(1, chips)
+            def _(k):
+                beside(k).wait_send()
+                across(k).wait_send()
+
+        return there, beside, combine, finish, sent
+
+    _, act_beside, act_combine, act_finish, act_sent = sum_copies(
+        1, act_out, act_pair, act_sum, act_in
+    )
+    hg_there, hg_beside, hg_combine, hg_finish, hg_sent = sum_copies(
+        4, hg_out, hg_pair, hg_sum, hg_in
+    )
+    hid_start, hid_forward, hid_finish, hid_sent = gather_copies(
+        2, hid16, lambda i: hid_in.at[i]
+    )
+    res_start, res_forward, res_finish, res_sent = gather_copies(
+        3, res16, lambda i: res_all.at[:, columns(i)]
+    )
+    tok_start, tok_forward, tok_finish, tok_sent = gather_copies(
+        5, tok16, lambda i: tok_all.at[:, columns(i)]
+    )
+
+    spare = wd.shape[1] // BLK - kept_count
+
+    def kept_block(ref, b):
+        shift = jnp.full((ref.shape[0], BLK), kept[b] - b, jnp.int32)
+        chosen = ref[:, b * BLK:(b + 1) * BLK].astype(f32)
+        for j in range(1, spare + 1):
+            other = ref[:, (b + j) * BLK:(b + j + 1) * BLK].astype(f32)
+            chosen = jnp.where(shift == j, other, chosen)
+        return chosen
+
+    def start_all(copy):
+        @pl.loop(1, n)
+        def _(k):
+            copy(k).start()
+
+    def receive_all(copy):
+        @pl.loop(1, n)
+        def _(k):
+            copy(k).wait_recv()
+
+    def sent_all(copy):
+        @pl.loop(1, n)
+        def _(k):
+            copy(k).wait_send()
+
+    start_all(pack_copy)
+    packs[me] = packed[:, columns(me)]
+    receive_all(pack_copy)
+    for s in range(n):
+        piece = packs[s].astype(f32)
+        tok32[s * mine:(s + 1) * mine, :] = piece[:mine]
+        tgt32[s * mine:(s + 1) * mine, :] = piece[mine:2 * mine]
+    tok16[...] = tok32[...].astype(bf16)
+    tok_start()
+
+    loads[0].wait()
+    loads[1].wait()
+    for half, weight in enumerate((wg, wu)):
+        here = pl.ds(half * rows, rows)
+        for c in range(0, weight.shape[1], 512):
+            full[here, c:c + 512] = jnp.dot(
+                tok16[...], weight[:, c:c + 512], preferred_element_type=f32
+            )
+    sel[:, kept_count * BLK:] = jnp.zeros((2 * rows, BLK), f32)
+    for b in range(kept_count):
+        sel[:, b * BLK:(b + 1) * BLK] = kept_block(full, b)
+    for p in range(n):
+        act_out[p] = sel[:, p * held:p * held + wide]
+
+    @pl.loop(1, chips)
+    def _(k):
+        act_beside(k).start()
+
+    act_beside(0).start()
+    act_combine()
+    tok_all[:, columns(me)] = tok16[...]
+
+    loads[2].wait()
+    down32[:, kept_count * BLK:] = jnp.zeros((features, BLK), f32)
+    for b in range(kept_count):
+        down32[:, b * BLK:(b + 1) * BLK] = kept_block(wd, b)
+    for p in range(n):
+        down[p] = down32[:, p * held:p * held + wide].astype(bf16)
+
+    tok_forward()
+    both = act_finish()
+    gate_act, up_act = both[:rows], both[rows:]
+    sigmoid_gate = jax.nn.sigmoid(gate_act)
+    silu_gate = gate_act * sigmoid_gate
+    inside = lax.broadcasted_iota(jnp.int32, (rows, wide), 1) < held
+    hidden = jnp.where(inside, silu_gate * up_act, 0.0).astype(bf16)
+    hid16[...] = hidden
+    hid_out[...] = hidden
+    hid_start()
+    hid_in[me] = hidden
+    tok32[...] = jnp.zeros((rows, features), f32)
+
+    def add_output(s):
+        tok32[...] += lax.dot_general(
+            hid_in[s], down[s], (((1,), (1,)), ((), ())), preferred_element_type=f32
+        )
+
+    add_output(me)
+    hid_forward(add_output)
+    hid_finish(add_output)
 
     output = jnp.zeros((rows, features), f32)
     for s in range(n):

time: 66.2 us -> 67.9 us (1.026)
  Pallas kernels: 56.6 us -> 58.1 us
    pallas_call x1, Pallas kernels: 56.6 us -> 58.1 us  [resident_weights_body(): pl.pallas_call(functools.partial(exchange_kernel, n, held), out_shape=(sm...]
where the time goes in v5:
time: 67.9 us; the launch traced here: 67.5 us
  Pallas kernels  58.1 us (86%)
  matrix products  7.07 us (10%)
  other arithmetic  1.51 us (2%)
  between operations  0.68 us (1%)
    pallas_call x1, Pallas kernels, resident_weights_body(): pl.pallas_call(functools.partial(exchange_kernel, n, held), out_shape=(sm...  58.1 us
    dot_general x3, matrix products, over_tokens(): lax.dot_general(left, right[:, :held], (((0,), (0,)), ((), ())), preferre...  7.07 us
    concatenate x1, other arithmetic, resident_weights_body(): packed = jnp.concatenate([tokens, target, filler], axis=0)  1.51 us

profile of v5, /device:TPU:0, one launch (start us, length us, event | category | flops | bytes accessed | tf_op | source)
XLA Modules:
  0.0 67.5 jit_solution(18122221378307448983)
XLA Ops:
  0.6 0.1 pad.2.clone
  0.7 1.5 %maximum_maximum_fusion.packed = bf16[16,4096]{1,0:T(8,128)(2,1)} fusion(bf16[4,4096]{1,0:T(4,128)(2,1)} %param.7, bf16[4,4096]{1,0:T(4,128)(2,1)} %param.6, bf16[16]{0:T(256)(128)(2,1)S(1)} %pad.2.clone), kind=kLoop, calls=%fused_computation.3 | loop fusion | flops 393216 | bytes 196640 | tf_op jit(solution)/shard_map/concatenate | solution.py:615
  2.2 58.1 %shard_map.85 = (bf16[64,256]{1,0:T(8,128)(2,1)}, bf16[64,256]{1,0:T(8,128)(2,1)}, bf16[64,256]{1,0:T(8,128)(2,1)}, bf16[64,4096]{1,0:T(8,128)(2,1)}, bf16[64,4096]{1,0:T(8,128)(2,1)}) custom-call(s32[30]{0:T(128)} %kept.1, bf16[16,4096]{1,0:T(8,128)(2,1)} %maximum_maximum_fusion.packed, bf16[256,4096]{1,0:T(8,128)(2,1)} %wg_hbm.1, ...), custom_call_target="tpu_custom_call" | custom-call | tf_op jit(solution)/shard_map/pallas_call | solution.py:622
  60.3 0.0 copy-start
  60.3 0.0 copy-start.3
  60.4 0.0 copy-start.1
  60.4 0.0 copy-start.2
  60.4 3.1 %convolution_convert_fusion.2 = bf16[4096,240]{0,1:T(8,128)(2,1)} fusion(bf16[64,4096]{1,0:T(8,128)(2,1)} %get-tuple-element.8, bf16[64,256]{1,0:T(8,128)(2,1)} %get-tuple-element.9), kind=kOutput, calls=%fused_computation.2 | convolution fusion | flops 126812160 | bytes 2523136 | tf_op jit(solution)/shard_map/dot_general | solution.py:660
  63.5 0.0 copy-done
  63.5 0.0 copy-done.3
  63.5 2.0 %convolution_convert_fusion.1 = bf16[4096,240]{0,1:T(8,128)(2,1)} fusion(bf16[64,4096]{1,0:T(8,128)(2,1)S(1)} %copy-done, bf16[64,256]{1,0:T(8,128)(2,1)S(1)} %copy-done.3), kind=kOutput, calls=%fused_computation.1 | convolution fusion | flops 126812160 | bytes 2523136 | tf_op jit(solution)/shard_map/dot_general | solution.py:660
  65.5 0.0 copy-done.1
  65.5 0.0 copy-done.2
  65.5 2.0 %convolution_convert_fusion = bf16[4096,240]{0,1:T(8,128)(2,1)} fusion(bf16[64,4096]{1,0:T(8,128)(2,1)S(1)} %copy-done.1, bf16[64,256]{1,0:T(8,128)(2,1)S(1)} %copy-done.2), kind=kOutput, calls=%fused_computation | convolution fusion | flops 126812160 | bytes 2523136 | tf_op jit(solution)/shard_map/dot_general | solution.py:660
  (1 shorter events, 0.0 us)
Async XLA Ops:
  60.3 3.1 %copy-start = (bf16[64,4096]{1,0:T(8,128)(2,1)S(1)}, bf16[64,4096]{1,0:T(8,128)(2,1)}, u32[]{:S(2)}) copy-start(bf16[64,4096]{1,0:T(8,128)(2,1)} %get-tuple-element.8) | copy-start | bytes 1572868
  60.3 3.1 %copy-start.3 = (bf16[64,256]{1,0:T(8,128)(2,1)S(1)}, bf16[64,256]{1,0:T(8,128)(2,1)}, u32[]{:S(2)}) copy-start(bf16[64,256]{1,0:T(8,128)(2,1)} %get-tuple-element.10) | copy-start | bytes 98308
  60.4 5.1 %copy-start.1 = (bf16[64,4096]{1,0:T(8,128)(2,1)S(1)}, bf16[64,4096]{1,0:T(8,128)(2,1)}, u32[]{:S(2)}) copy-start(bf16[64,4096]{1,0:T(8,128)(2,1)} %get-tuple-element.11) | copy-start | bytes 1572868
  60.4 5.1 %copy-start.2 = (bf16[64,256]{1,0:T(8,128)(2,1)S(1)}, bf16[64,256]{1,0:T(8,128)(2,1)}, u32[]{:S(2)}) copy-start(bf16[64,256]{1,0:T(8,128)(2,1)} %get-tuple-element.12) | copy-start | bytes 98308

commit v6 on v4

--- a/solution.py
+++ b/solution.py
@@ -168,14 +168,16 @@
             j = there(k)
             return remote(phase, chips + k, total.at[j], landed.at[chip], 2 * j + core)
 
-        def combine():
+        def combine(prepare=lambda i: None):
             @pl.loop(1, chips)
             def _(k):
                 j = there(k)
+                prepare(2 * j + core)
                 beside(k).wait_recv()
                 total[j] = (out[2 * j + core] + pair[j]).astype(bf16)
                 across(k).start()
 
+            prepare(me)
             beside(0).wait_recv()
             landed[chip] = (out[me] + pair[chip]).astype(bf16)
 
@@ -310,11 +312,7 @@
         hg_piece(2 * hg_there(k) + 1 - core)
         hg_beside(k).start()
 
-    @pl.loop(0, chips)
-    def _(k):
-        hg_piece(2 * hg_there(k) + core)
-
-    hg_combine()
+    hg_combine(hg_piece)
     res_start()
     res_all[:, columns(me)] = residual
     res_forward()

time: 66.2 us -> 66 us (level)
  no operation moved by 1% of the time
where the time goes in v6:
time: 66 us; the launch traced here: 65.5 us
  Pallas kernels  56.1 us (85%)
  matrix products  7.07 us (11%)
  other arithmetic  1.51 us (2%)
  between operations  0.68 us (1%)
    pallas_call x1, Pallas kernels, resident_weights_body(): pl.pallas_call(functools.partial(exchange_kernel, n, held), out_shape=(sm...  56.1 us
    dot_general x3, matrix products, over_tokens(): lax.dot_general(left, right[:, :held], (((0,), (0,)), ((), ())), preferre...  7.07 us
    concatenate x1, other arithmetic, resident_weights_body(): packed = jnp.concatenate([tokens, target, filler], axis=0)  1.51 us

profile of v6, /device:TPU:0, one launch (start us, length us, event | category | flops | bytes accessed | tf_op | source)
XLA Modules:
  0.0 65.5 jit_solution(17474155758457359213)
XLA Ops:
  0.6 0.1 pad.2.clone
  0.7 1.5 %maximum_maximum_fusion.packed = bf16[16,4096]{1,0:T(8,128)(2,1)} fusion(bf16[4,4096]{1,0:T(4,128)(2,1)} %param.7, bf16[4,4096]{1,0:T(4,128)(2,1)} %param.6, bf16[16]{0:T(256)(128)(2,1)S(1)} %pad.2.clone), kind=kLoop, calls=%fused_computation.3 | loop fusion | flops 393216 | bytes 196640 | tf_op jit(solution)/shard_map/concatenate | solution.py:341
  2.2 56.1 %shard_map.85 = (bf16[64,256]{1,0:T(8,128)(2,1)}, bf16[64,256]{1,0:T(8,128)(2,1)}, bf16[64,256]{1,0:T(8,128)(2,1)}, bf16[64,4096]{1,0:T(8,128)(2,1)}, bf16[64,4096]{1,0:T(8,128)(2,1)}) custom-call(s32[30]{0:T(128)} %kept.1, bf16[16,4096]{1,0:T(8,128)(2,1)} %maximum_maximum_fusion.packed, bf16[256,4096]{1,0:T(8,128)(2,1)} %wg_hbm.1, ...), custom_call_target="tpu_custom_call" | custom-call | tf_op jit(solution)/shard_map/pallas_call | solution.py:348
  58.4 0.0 copy-start
  58.4 0.0 copy-start.3
  58.4 0.0 copy-start.1
  58.4 0.0 copy-start.2
  58.4 3.1 %convolution_convert_fusion.2 = bf16[4096,240]{0,1:T(8,128)(2,1)} fusion(bf16[64,4096]{1,0:T(8,128)(2,1)} %get-tuple-element.8, bf16[64,256]{1,0:T(8,128)(2,1)} %get-tuple-element.9), kind=kOutput, calls=%fused_computation.2 | convolution fusion | flops 126812160 | bytes 2523136 | tf_op jit(solution)/shard_map/dot_general | solution.py:386
  61.5 0.0 copy-done
  61.5 0.0 copy-done.3
  61.5 2.0 %convolution_convert_fusion.1 = bf16[4096,240]{0,1:T(8,128)(2,1)} fusion(bf16[64,4096]{1,0:T(8,128)(2,1)S(1)} %copy-done, bf16[64,256]{1,0:T(8,128)(2,1)S(1)} %copy-done.3), kind=kOutput, calls=%fused_computation.1 | convolution fusion | flops 126812160 | bytes 2523136 | tf_op jit(solution)/shard_map/dot_general | solution.py:386
  63.5 0.0 copy-done.1
  63.5 0.0 copy-done.2
  63.5 2.0 %convolution_convert_fusion = bf16[4096,240]{0,1:T(8,128)(2,1)} fusion(bf16[64,4096]{1,0:T(8,128)(2,1)S(1)} %copy-done.1, bf16[64,256]{1,0:T(8,128)(2,1)S(1)} %copy-done.2), kind=kOutput, calls=%fused_computation | convolution fusion | flops 126812160 | bytes 2523136 | tf_op jit(solution)/shard_map/dot_general | solution.py:386
  (1 shorter events, 0.0 us)
Async XLA Ops:
  58.4 3.1 %copy-start = (bf16[64,4096]{1,0:T(8,128)(2,1)S(1)}, bf16[64,4096]{1,0:T(8,128)(2,1)}, u32[]{:S(2)}) copy-start(bf16[64,4096]{1,0:T(8,128)(2,1)} %get-tuple-element.8) | copy-start | bytes 1572868
  58.4 3.1 %copy-start.3 = (bf16[64,256]{1,0:T(8,128)(2,1)S(1)}, bf16[64,256]{1,0:T(8,128)(2,1)}, u32[]{:S(2)}) copy-start(bf16[64,256]{1,0:T(8,128)(2,1)} %get-tuple-element.10) | copy-start | bytes 98308
  58.4 5.1 %copy-start.1 = (bf16[64,4096]{1,0:T(8,128)(2,1)S(1)}, bf16[64,4096]{1,0:T(8,128)(2,1)}, u32[]{:S(2)}) copy-start(bf16[64,4096]{1,0:T(8,128)(2,1)} %get-tuple-element.11) | copy-start | bytes 1572868
  58.4 5.1 %copy-start.2 = (bf16[64,256]{1,0:T(8,128)(2,1)S(1)}, bf16[64,256]{1,0:T(8,128)(2,1)}, u32[]{:S(2)}) copy-start(bf16[64,256]{1,0:T(8,128)(2,1)} %get-tuple-element.12) | copy-start | bytes 98308
